TPU v7x, 32 devices: a whole 2x2x4 slice. The times are simulated.
32 devices in a mesh: group: 4 (over y, core), member: 8 (over z, x).
Axes of the slice: x: 2, y: 2, z: 4, core: 2. Of those that a mesh axis runs over, the one named last changes fastest.
Arguments:
- fine_blocks: float32 [512, 5, 128, 128], P(('group', 'member')), may hold values from -6 to 6
- neighbours: int32 [512, 5], P(('group', 'member')), may hold values from 0 to 511, as said below
- slot_one: int32 [512, 5], P(('group', 'member')), may hold values from 0 to 4
- pair_one: int32 [512], P(('group', 'member')), may hold values from 0 to 255, as said below
- prolong_one: float32 [128, 128], replicated, may hold values from -0.5 to 0.5
- slot_two: int32 [256, 5], P(('group', 'member')), may hold values from 0 to 4
- pair_two: int32 [256], P(('group', 'member')), may hold values from 0 to 127, as said below
- prolong_two: float32 [128, 128], replicated, may hold values from -0.5 to 0.5
- diag_inverse: float32 [512, 128, 128], P(('group', 'member')), may hold values from -0.01953125 to 0.01953125
- right_side: float32 [512, 128], P(('group', 'member')), may hold values from -96 to 96
- initial_guess: float32 [512, 128], P(('group', 'member')), may hold values from -6 to 6
Outputs:
- coarse_one: float32 [256, 5, 128, 128], P(('group', 'member'))
- coarse_two: float32 [128, 5, 128, 128], P(('group', 'member'))
- smoothed: float32 [512, 128], P(('group', 'member'))
Inputs may be any that keep to these rules, and one draw needn't show every extreme that they name: Entry 0 of a row is the row's own element; the other four are its neighbours on a periodic grid and lie in the rows of the same device or of the devices just before and just after it in group-major order, cyclically. `pair_one`: every first-level coarse row is named by exactly two fine elements. A fine element names a coarse row held by a device of its own group; the rows of one device name at most 4 rows held by any one device, and some device names exactly 4 rows of some device. `pair_two`: every second-level coarse row is named by exactly two first-level rows. A first-level row names a row held by a device with the same member index; the rows of one device name at most 4 rows held by any one device, and some device names exactly 4 rows of some device.
All inputs are finite; a program needn't handle non-finite values.
Results may differ from a plain program's by a relative error of at most 0.0001.
Values sent between devices are 32-bit elements; how exact they have to be, the bound alone decides.
No kernel may reach another device: no remote copies, remote signals or barrier semaphores. Data moves between devices by JAX's collectives and lax.ppermute only.
A program may use at most 128 MiB of HBM per device.

v0:
```python
import functools

import jax
import jax.numpy as jnp
from jax import lax
from jax.experimental import pallas as pl
from jax.experimental.pallas import tpu as pltpu
from jax.sharding import PartitionSpec as P

damping = 0.7
rows_a_step = 4
prepare_limit = 20 * 1024 * 1024
vmem_limit = 20 * 1024 * 1024
pause = 3
beside = 6


def grid_of(member_count):
    x_count = max(d for d in range(1, member_count + 1) if member_count % d == 0 and d * d <= member_count)
    return member_count // x_count, x_count


def chunk_steps(part):
    tiles = part // 8
    step = max(tiles // 4, 1)
    ends = [max(step // 2, 1)] * min(2, tiles)
    inner = tiles - sum(ends)
    steps = ends[:1] + [step] * (inner // step) + [inner % step] * (inner % step > 0) + ends[1:]
    return [8 * step for step in steps]


def split(values):
    high = values.astype(jnp.bfloat16)
    low = (values - high.astype(jnp.float32)).astype(jnp.bfloat16)
    return high, low


def load_weights(prolong_ref, left_ref, right_ref):
    prolong = prolong_ref[...]
    size = prolong.shape[0]
    high, low = split(prolong)
    high_t, low_t = split(prolong.T)
    for half in range(2):
        at = pl.ds(half * size, size)
        left_ref[0:size, at] = high_t
        left_ref[size : 2 * size, at] = low_t
        right_ref[at, 0:size] = high
        right_ref[at, size : 2 * size] = low


def triple(blocks, left_ref, right_ref):
    size = blocks[0].shape[0]
    count = len(blocks)
    high, low = split(jnp.concatenate(blocks, axis=1))
    both = jnp.dot(
        left_ref[...], jnp.concatenate([high, low], axis=0), preferred_element_type=jnp.float32
    )
    left = both[:size] + both[size:]
    rows = jnp.concatenate([left[:, s * size : (s + 1) * size] for s in range(count)], axis=0)
    high, low = split(rows)
    both = jnp.dot(
        jnp.concatenate([high, low], axis=1), right_ref[...], preferred_element_type=jnp.float32
    )
    return (both[:, :size] + both[:, size:]).reshape(count, size, size)


def prepare_kernel(x_count, slot_ref, place_ref, prolong_ref, fine_ref, *rest):
    outs, (left_ref, right_ref, sums_ref, done_ref) = rest[:-4], rest[-4:]
    held, links, size, _ = fine_ref.shape
    chunks = len(outs) // x_count
    part = size // x_count

    @pl.when(pl.program_id(0) == 0)
    def _():
        load_weights(prolong_ref, left_ref, right_ref)

    sums_ref[...] = jnp.zeros_like(sums_ref)
    for row in range(held):
        for link in range(links):
            slot = slot_ref[pl.program_id(0) * held + row, link]
            sums_ref[row, slot] += fine_ref[row, link]
    sums = [sums_ref[row, slot] for row in range(held) for slot in range(links)]
    done_ref[...] = triple(sums, left_ref, right_ref).reshape(done_ref.shape)
    for offset in range(x_count):
        start = lax.rem(place_ref[0] + offset, x_count) * part
        for out in outs[offset * chunks : (offset + 1) * chunks]:
            step = out.shape[2]
            out[...] = done_ref[:, :, pl.ds(pl.multiple_of(start, 8), step), :]
            start = start + step


def prepare(fine_blocks, slot_one, prolong_one, place, x_count, steps):
    rows, links, size, _ = fine_blocks.shape
    chunks = len(steps)
    held = max(h for h in range(1, rows_a_step + 1) if rows % h == 0)
    outs = pl.pallas_call(
        functools.partial(prepare_kernel, x_count),
        out_shape=[
            jax.ShapeDtypeStruct((rows, links, step, size), jnp.float32)
            if chunk < 2
            else pltpu.HBM((rows, links, step, size), jnp.float32)
            for chunk, step in enumerate(steps)
        ]
        * x_count,
        grid_spec=pltpu.PrefetchScalarGridSpec(
            num_scalar_prefetch=2,
            grid=(rows // held,),
            in_specs=[
                pl.BlockSpec((size, size), lambda e, *_: (0, 0)),
                pl.BlockSpec((held, links, size, size), lambda e, *_: (e, 0, 0, 0)),
            ],
            out_specs=[
                pl.BlockSpec((held, links, step, size), lambda e, *_: (e, 0, 0, 0)) for step in steps
            ]
            * x_count,
            scratch_shapes=[
                pltpu.VMEM((2 * size, 2 * size), jnp.bfloat16),
                pltpu.VMEM((2 * size, 2 * size), jnp.bfloat16),
                pltpu.VMEM((held, links, size, size), jnp.float32),
                pltpu.VMEM((held, links, size, size), jnp.float32),
            ],
        ),
        compiler_params=pltpu.CompilerParams(vmem_limit_bytes=prepare_limit),
        cost_estimate=pl.CostEstimate(
            flops=16 * rows * links * size**3,
            bytes_accessed=8 * rows * links * size**2,
            transcendentals=0,
        ),
        name="prepare",
    )(slot_one, place, prolong_one, fine_blocks)
    return [list(outs[offset * chunks : (offset + 1) * chunks]) for offset in range(x_count)]


def whole(kernel, scalars, arrays, out_shapes, name, work=0, scratch=()):
    return pl.pallas_call(
        kernel,
        out_shape=out_shapes,
        in_specs=[pl.BlockSpec(memory_space=pltpu.SMEM)] * len(scalars)
        + [pl.BlockSpec(memory_space=pltpu.VMEM)] * len(arrays),
        out_specs=[pl.BlockSpec(memory_space=pltpu.VMEM)] * len(out_shapes),
        scratch_shapes=scratch,
        compiler_params=pltpu.CompilerParams(vmem_limit_bytes=vmem_limit),
        cost_estimate=pl.CostEstimate(flops=work * 10**9, bytes_accessed=0, transcendentals=0),
        name=name,
    )(*scalars, *arrays)


def combine_kernel(sources, target_ref, *refs):
    arrays, (far_ref, sums_ref) = refs[:sources], refs[sources:]
    rows = arrays[0].shape[0]
    sums_ref[...] = jnp.zeros_like(sums_ref)
    for source in range(sources):

        def one(row, carry, source=source):
            sums_ref[target_ref[source, row]] += arrays[source][row]
            return carry

        lax.fori_loop(0, rows, one, 0, unroll=True)
    far_ref[...] = sums_ref[0 : far_ref.shape[0]]


def finish_kernel(middle_ref, sums_ref, got_ref, *outs):
    half, rows = got_ref.shape[0], outs[-1].shape[0]
    own = len([out for out in outs if out.shape[0] == rows])
    far, near = outs[:-own], outs[-own:]
    width = own * rows
    for d, out in enumerate(far):
        at = (d + 1) * width
        out[...] = sums_ref[half + at : half + at + width] + got_ref[at : at + width]
    for offset, out in enumerate(near):
        at = offset * rows
        total = sums_ref[half + at : half + at + rows] + got_ref[at : at + rows]
        out[...] = jnp.where(middle_ref[0] > 0, total, 0.0)


def settle_kernel(count, *refs):
    near, far, outs = refs[:count], refs[count:-count], refs[-count:]
    rows = outs[0].shape[0]
    for offset, out in enumerate(outs):
        total = near[offset][...]
        for piece in far:
            total = total + piece[offset * rows : (offset + 1) * rows]
        out[...] = total


def second_kernel(x_count, slot_ref, target_ref, *refs):
    parts, outs, sums_ref = refs[:x_count], refs[x_count:-1], refs[-1]
    rows, links, step, _ = parts[0].shape
    share = outs[0].shape[0]
    sums_ref[...] = jnp.zeros_like(sums_ref)

    def one(row, carry):
        target = target_ref[row]
        for link in range(links):
            slot = slot_ref[row, link]
            for offset, part in enumerate(parts):
                sums_ref[target, slot, offset * step : (offset + 1) * step, :] += part[row, link]
        return carry

    lax.fori_loop(0, rows, one, 0, unroll=True)
    for way, out in enumerate(outs):
        out[...] = sums_ref[way * share : (way + 1) * share]


def place_kernel(x_count, place_ref, *refs):
    pieces, out = refs[:-1], refs[-1]
    part = out.shape[2] // x_count
    chunks = len(pieces) // x_count
    for offset in range(x_count):
        start = lax.rem(place_ref[0] + x_count - offset, x_count) * part
        for piece in pieces[offset * chunks : (offset + 1) * chunks]:
            step = piece.shape[2]
            out[:, :, pl.ds(pl.multiple_of(start, 8), step), :] = piece[...]
            start = start + step


def place_one(pieces, place, x_count):
    rows, links, _, size = pieces[0].shape
    return pl.pallas_call(
        functools.partial(place_kernel, x_count),
        out_shape=jax.ShapeDtypeStruct((rows, links, size, size), jnp.float32),
        grid_spec=pltpu.PrefetchScalarGridSpec(
            num_scalar_prefetch=1,
            grid=(rows,),
            in_specs=[
                pl.BlockSpec((1, links, piece.shape[2], size), lambda e, *_: (e, 0, 0, 0))
                for piece in pieces
            ],
            out_specs=pl.BlockSpec((1, links, size, size), lambda e, *_: (e, 0, 0, 0)),
        ),
        compiler_params=pltpu.CompilerParams(vmem_limit_bytes=vmem_limit),
        cost_estimate=pl.CostEstimate(
            flops=0, bytes_accessed=8 * rows * links * size**2, transcendentals=0
        ),
        name="place_one",
    )(place, *pieces)


def last_kernel(x_count, peers, place_ref, prolong_ref, *refs):
    pieces, (out, left_ref, right_ref, sums_ref) = refs[:-4], refs[-4:]
    links, size = out.shape[1], out.shape[2]
    part = size // x_count

    @pl.when(pl.program_id(0) == 0)
    def _():
        load_weights(prolong_ref, left_ref, right_ref)

    done = 0
    for first in range(0, len(pieces), peers):
        total = pieces[first][...]
        for piece in pieces[first + 1 : first + peers]:
            total = total + piece[...]
        step = total.shape[2] // x_count
        for offset in range(x_count):
            start = lax.rem(place_ref[0] + x_count - offset, x_count) * part
            at = pl.multiple_of(start + done, 8)
            sums_ref[:, :, pl.ds(at, step), :] = total[:, :, offset * step : (offset + 1) * step, :]
        done += step
    sums = [sums_ref[row, slot] for row in range(out.shape[0]) for slot in range(links)]
    out[...] = triple(sums, left_ref, right_ref).reshape(out.shape)


def last(pieces, prolong_two, place, x_count, peers):
    rows, links, _, size = pieces[0].shape
    held = max(h for h in range(1, rows_a_step // 2 + 1) if rows % h == 0)
    return pl.pallas_call(
        functools.partial(last_kernel, x_count, peers),
        out_shape=jax.ShapeDtypeStruct((rows, links, size, size), jnp.float32),
        grid_spec=pltpu.PrefetchScalarGridSpec(
            num_scalar_prefetch=1,
            grid=(rows // held,),
            in_specs=[pl.BlockSpec((size, size), lambda e, *_: (0, 0))]
            + [
                pl.BlockSpec((held, links, piece.shape[2], size), lambda e, *_: (e, 0, 0, 0))
                for piece in pieces
            ],
            out_specs=pl.BlockSpec((held, links, size, size), lambda e, *_: (e, 0, 0, 0)),
            scratch_shapes=[
                pltpu.VMEM((2 * size, 2 * size), jnp.bfloat16),
                pltpu.VMEM((2 * size, 2 * size), jnp.bfloat16),
                pltpu.VMEM((held, links, size, size), jnp.float32),
            ],
        ),
        compiler_params=pltpu.CompilerParams(vmem_limit_bytes=vmem_limit),
        cost_estimate=pl.CostEstimate(
            flops=16 * rows * links * size**3,
            bytes_accessed=4 * rows * links * size**2 * (peers + 1),
            transcendentals=0,
        ),
        name="last",
    )(place, prolong_two, *pieces)


def around(initial_guess):
    axes = ("group", "member")
    devices = lax.axis_size(axes)
    before = lax.ppermute(initial_guess, axes, [(i, (i + 1) % devices) for i in range(devices)])
    after = lax.ppermute(initial_guess, axes, [(i, (i - 1) % devices) for i in range(devices)])
    return [before, initial_guess, after]


def sweep(fine_blocks, neighbours, diag_inverse, right_side, initial_guess, window):
    rows = fine_blocks.shape[0]
    axes = ("group", "member")
    devices = lax.axis_size(axes)
    device = lax.axis_index(axes)
    window = jnp.concatenate(window, axis=0)
    position = (neighbours - device * rows + rows) % (rows * devices)
    nearby = window[position]
    product = jnp.sum(fine_blocks * nearby[:, :, None, :], axis=(1, 3))
    defect = right_side - product
    return initial_guess + damping * jnp.sum(diag_inverse * defect[:, None, :], axis=2)


def local(
    fine_blocks,
    neighbours,
    slot_one,
    pair_one,
    prolong_one,
    slot_two,
    pair_two,
    prolong_two,
    diag_inverse,
    right_side,
    initial_guess,
):
    rows, links, size, _ = fine_blocks.shape
    rows_one, rows_two = rows // 2, rows // 4
    members, groups = lax.axis_size("member"), lax.axis_size("group")
    z_count, x_count = grid_of(members)
    half = z_count // 2
    part = size // x_count
    steps = chunk_steps(part)

    member = lax.axis_index("member")
    z, x = member // x_count, member % x_count
    upper = (z >= half).astype(jnp.int32)
    place = jnp.stack([x]).astype(jnp.int32)

    def at(side, d, x_at):
        return (half + d if side else half - 1 - d) * x_count + x_at % x_count

    def hop(array, d_from, d_to, offset):
        pairs = [
            (at(side, d_from, x_at), at(side, d_to, x_at + offset))
            for side in range(2)
            for x_at in range(x_count)
        ]
        return lax.ppermute(array, "member", pairs)

    def hop_x(array, offset):
        pairs = [
            (z_at * x_count + x_at, z_at * x_count + (x_at + offset) % x_count)
            for z_at in range(z_count)
            for x_at in range(x_count)
        ]
        return lax.ppermute(array, "member", pairs)

    routes = [(d, o) for d in range(half) for o in range(x_count)]

    def along(arrays):
        return [array if o == 0 else hop_x(array, o) for o, array in enumerate(arrays)]

    def inward(arrays):
        return arrays + [hop(array, d, 0, 0) for d in range(1, half) for array in arrays]

    tags = jnp.stack(along([pair_one] * x_count))
    slot_one, tags, window = lax.optimization_barrier((slot_one, tags, around(initial_guess)))
    owner_rows = jnp.concatenate([tags] + [hop(tags, d, 0, 0) for d in range(1, half)])
    owner = owner_rows // rows_one % members
    owner_z, owner_x = owner // x_count, owner % x_count
    owner_upper = (owner_z >= half).astype(jnp.int32)
    owner_d = jnp.where(owner_upper > 0, owner_z - half, half - 1 - owner_z)
    near = (owner_upper == upper).astype(jnp.int32)
    target_one = ((near * half + owner_d) * x_count + (owner_x - x + x_count) % x_count) * rows_one
    target_one = (target_one + owner_rows % rows_one).astype(jnp.int32)
    middle = jnp.stack([(z == half - 1) | (z == half)]).astype(jnp.int32)

    way = (pair_two // rows_two // members - lax.axis_index("group") + groups) % groups
    target_two = (way * rows_two + pair_two % rows_two).astype(jnp.int32)

    outgoing = prepare(fine_blocks, slot_one, prolong_one, place, x_count, steps)
    across = [(at(0, 0, x_at), at(1, 0, x_at)) for x_at in range(x_count)]
    across = across + [(b, a) for a, b in across]
    before = [target_one]

    def in_turn(kernel, scalars, arrays, out_shapes, name, **more):
        arrays, before[0] = lax.optimization_barrier((list(arrays), before[0]))
        outs = whole(kernel, scalars, arrays, out_shapes, name, **more)
        before[0] = outs[0]
        return outs

    def rows_of(count, height):
        return jax.ShapeDtypeStruct((count, links, height, size), jnp.float32)

    coming, targets = [], [target_one]
    for chunk in range(len(steps)):
        own = outgoing[0][chunk]
        if chunk > 0:
            ahead = coming[-1]
            tied = (own, ahead[x_count], targets[0]) if chunk == 1 else (own, ahead[x_count])
            own, ahead[x_count], *seen = lax.optimization_barrier(tied)
            targets += seen
        coming.append(inward(along([own] + [ways[chunk] for ways in outgoing[1:]])))
    received = []

    smoothed = []

    def combine(chunk):
        held = coming[chunk]
        if chunk == min(1, len(steps) - 1):
            later, before[0] = lax.optimization_barrier((neighbours, before[0]))
            swept = sweep(fine_blocks, later, diag_inverse, right_side, initial_guess, window)
            held, swept = lax.optimization_barrier((held, swept))
            smoothed.append(swept)
        total = half * x_count * rows_one
        far, kept = in_turn(
            functools.partial(combine_kernel, len(held)),
            [targets[min(chunk, 1)]],
            held,
            [rows_of(total, steps[chunk]), rows_of(2 * total, steps[chunk])],
            "combine",
            work=beside,
        )
        return kept, lax.ppermute(far, "member", across)

    def finish(chunk, sums):
        finished = in_turn(
            finish_kernel,
            [middle],
            sums,
            [rows_of(x_count * rows_one, steps[chunk])] * (half - 1)
            + [rows_of(rows_one, steps[chunk])] * x_count,
            "finish",
        )
        return list(finished[half - 1 :]) + [hop(finished[d - 1], 0, d, 0) for d in range(1, half)]

    def settle(chunk, finished):
        if chunk == 0 and len(steps) > 2:
            ahead = coming[chunk + 2]
            ahead[x_count], finished = lax.optimization_barrier((ahead[x_count], finished))
        return along(
            in_turn(
                functools.partial(settle_kernel, x_count),
                [],
                finished,
                [rows_of(rows_one, steps[chunk])] * x_count,
                "settle",
            )
        )

    def second(chunk, ours):
        received[-groups:], ours = lax.optimization_barrier((received[-groups:], ours))
        height = x_count * steps[chunk]
        shares = in_turn(
            functools.partial(second_kernel, x_count),
            [slot_two, target_two],
            ours,
            [rows_of(rows_two, height)] * groups,
            "second",
            scratch=[pltpu.VMEM((groups * rows_two, links, height, size), jnp.float32)],
        )
        for way, share in enumerate(shares):
            circle = [(g, (g + way) % groups) for g in range(groups)]
            received.append(lax.ppermute(share, "group", circle) if way > 0 else share)
        return ours

    stages, shares = (combine, finish, settle, second), (1.0, 0.5, 0.25)
    turns, rows_in, swapped = [], 0.0, 0.0
    for chunk, step in enumerate(steps):
        rows_in += step
        time = swapped = max(rows_in, swapped) + step + pause
        turns += [(rows_in, 0, chunk), (time, 1, chunk)]
        for stage, share in enumerate(shares[1:], 2):
            time += share * step + pause
            turns.append((time, stage, chunk))
    held = [[None] * len(steps) for _ in range(len(stages) + 1)]
    for _, stage, chunk in sorted(turns):
        given = [held[stage][chunk]] if stage > 0 else []
        held[stage + 1][chunk] = stages[stage](chunk, *given)
    parts = held[4]

    coarse_one = place_one(
        [parts[chunk][o] for o in range(x_count) for chunk in range(len(steps))], place, x_count
    )
    coarse_two = last(received, prolong_two, place, x_count, groups)
    return (coarse_one, coarse_two, smoothed[0])


def solution(mesh):
    rows = P(("group", "member"))
    return jax.shard_map(
        local,
        mesh=mesh,
        in_specs=(rows, rows, rows, rows, P(), rows, rows, P(), rows, rows, rows),
        out_specs=(rows, rows, rows),
        check_vma=False,
    )
```

profile of v0, /device:TPU:0, one launch (start us, length us, event | category | flops | bytes accessed | tf_op | source)
XLA Modules:
  0.0 225.2 jit_solution(16580201313896343896)
XLA Ops:
  0.6 3.0 %collective-permute-start.1 = (f32[16,128]{1,0:T(8,128)}, f32[16,128]{1,0:T(8,128)S(1)}, u32[]{:S(2)}, u32[]{:S(2)}) collective-permute-start(f32[16,128]{1,0:T(8,128)} %param.21), channel_id=1, source_target_pairs={{0,1},{1,2},{2,3},{3,4},{4,5},{5,6},{6,7},{7,8},{8,9},{9,10},{10,1... | collective-permute-start | bytes 24584 | tf_op jit(solution)/shard_map/ppermute | solution.py:297
  3.6 3.5 %collective-permute-start.2 = (f32[16,128]{1,0:T(8,128)}, f32[16,128]{1,0:T(8,128)S(1)}, u32[]{:S(2)}, u32[]{:S(2)}) collective-permute-start(f32[16,128]{1,0:T(8,128)} %param.21), channel_id=1, source_target_pairs={{0,31},{1,0},{2,1},{3,2},{4,3},{5,4},{6,5},{7,6},{8,7},{9,8},{10,9... | collective-permute-start | bytes 24584 | tf_op jit(solution)/shard_map/ppermute | solution.py:298
  7.1 3.7 %collective-permute-done = s32[16]{0:T(128)S(1)} collective-permute-done((s32[16]{0:T(128)}, s32[16]{0:T(128)S(1)}, u32[]{:S(2)}, u32[]{:S(2)}) %collective-permute-start) | collective-permute-done | bytes 96 | tf_op jit(solution)/shard_map/ppermute | solution.py:358
  12.3 2.5 %copy-done = f32[16,5,128,128]{3,2,1,0:T(8,128)S(1)} copy-done((f32[16,5,128,128]{3,2,1,0:T(8,128)S(1)}, f32[16,5,128,128]{3,2,1,0:T(8,128)}, u32[]{:S(2)}) %copy-start) | copy-done | bytes 5242904
  15.6 7.1 %prepare.1 = (f32[16,5,8,128]{3,2,1,0:T(8,128)S(1)}, f32[16,5,16,128]{3,2,1,0:T(8,128)}, f32[16,5,16,128]{3,2,1,0:T(8,128)}, f32[16,5,16,128]{3,2,1,0:T(8,128)},...) custom-call(s32[16,5]{1,0:T(8,128)S(1)} %copy.16.slot_ref, ...), custom_call_target="tpu_custom_call" | custom-call | flops 2684354560 | bytes 10485760 | tf_op jit(solution)/shard_map/prepare/pallas_call | solution.py:96
  22.7 2.0 collective-permute-start.3
  24.7 6.2 %collective-permute-done.7.refs_1_ = f32[16,5,8,128]{3,2,1,0:T(8,128)S(1)} collective-permute-done((f32[16,5,8,128]{3,2,1,0:T(8,128)S(1)}, f32[16,5,8,128]{3,2,1,0:T(8,128)S(1)}, u32[]{:S(2)}, u32[]{:S(2)}) %collective-permute-start.7) | collective-permute-done | bytes 327712 | tf_op jit(solution)/shard_map/ppermute | solution.py:358
  30.9 1.3 collective-permute-start.8
  34.2 3.2 %collective-permute-done.4 = s32[2,16]{1,0:T(2,128)S(1)} collective-permute-done((s32[2,16]{1,0:T(2,128)S(1)}, s32[2,16]{1,0:T(2,128)S(1)}, u32[]{:S(2)}, u32[]{:S(2)}) %collective-permute-start.4) | collective-permute-done | bytes 160 | tf_op jit(solution)/shard_map/ppermute | solution.py:350
  37.4 5.4 %collective-permute-start.5 = (f32[16,5,16,128]{3,2,1,0:T(8,128)}, f32[16,5,16,128]{3,2,1,0:T(8,128)}, u32[]{:S(2)}, u32[]{:S(2)}) collective-permute-start(f32[16,5,16,128]{3,2,1,0:T(8,128)} %get-tuple-element.209.refs_0_), channel_id=1, source_target_pairs={{0,2},{1,3},{6,4},{7,5},{8,10},{9,11},{14,12},{15,13},{16,18},{17,... | collective-permute-start | bytes 1966088 | tf_op jit(solution)/shard_map/ppermute | solution.py:350
  42.8 1.9 combine.5
  45.6 1.4 collective-permute-start.18
  47.1 3.3 %collective-permute-done.11.refs_1_ = f32[16,5,16,128]{3,2,1,0:T(8,128)} collective-permute-done((f32[16,5,16,128]{3,2,1,0:T(8,128)}, f32[16,5,16,128]{3,2,1,0:T(8,128)}, u32[]{:S(2)}, u32[]{:S(2)}) %collective-permute-start.11) | collective-permute-done | bytes 655392 | tf_op jit(solution)/shard_map/ppermute | solution.py:358
  50.4 3.4 %collective-permute-start.12 = (f32[16,5,16,128]{3,2,1,0:T(8,128)}, f32[16,5,16,128]{3,2,1,0:T(8,128)}, u32[]{:S(2)}, u32[]{:S(2)}) collective-permute-start(f32[16,5,16,128]{3,2,1,0:T(8,128)} %collective-permute-done.11.refs_1_), channel_id=1, source_target_pairs={{0,2},{1,3},{6,4},{7,5},{8,10},{9,11},{14,12},{15,13},{16,18},{17,... | collective-permute-start | bytes 1966088 | tf_op jit(solution)/shard_map/ppermute | solution.py:350
  54.3 5.2 %collective-permute-start.6 = (f32[16,5,16,128]{3,2,1,0:T(8,128)S(1)}, f32[16,5,16,128]{3,2,1,0:T(8,128)}, u32[]{:S(2)}, u32[]{:S(2)}) collective-permute-start(f32[16,5,16,128]{3,2,1,0:T(8,128)S(1)} %copy-done.4), channel_id=1, source_target_pairs={{0,2},{1,3},{6,4},{7,5},{8,10},{9,11},{14,12},{15,13},{16,18},{17,... | collective-permute-start | bytes 1966088 | tf_op jit(solution)/shard_map/ppermute | solution.py:350
  60.5 3.0 %multiply_reduce_fusion = f32[16,128]{1,0:T(8,128)S(1)} fusion(f32[16,5,128,128]{3,2,1,0:T(8,128)} %fine_ref.1, f32[16,5,128]{2,1,0:T(8,128)S(1)} %reshape.12), kind=kLoop, calls=%fused_computation.1 | loop fusion | flops 2619392 | bytes 5292032 | tf_op jit(solution)/shard_map/reduce_sum | solution.py:310
  64.5 3.9 %collective-permute-done.12.refs_3_ = f32[16,5,16,128]{3,2,1,0:T(8,128)} collective-permute-done((f32[16,5,16,128]{3,2,1,0:T(8,128)}, f32[16,5,16,128]{3,2,1,0:T(8,128)}, u32[]{:S(2)}, u32[]{:S(2)}) %collective-permute-start.12) | collective-permute-done | bytes 655392 | tf_op jit(solution)/shard_map/ppermute | solution.py:350
  68.4 2.4 %combine.6 = (f32[32,5,16,128]{3,2,1,0:T(8,128)S(1)}, f32[64,5,16,128]{3,2,1,0:T(8,128)S(1)}) custom-call(s32[4,16]{1,0:T(4,128)S(1)} %fusion.7.target_ref, f32[16,5,16,128]{3,2,1,0:T(8,128)} %get-tuple-element.209.refs_0_, f32[16,5,16,128]{3,2,1,0:T(8,128)} %collective-permute-done.11.refs_1_, f32[16,5,16,128]{3,2,1,0:T(8,128)} %collective-permute-done.5.refs_2_, ...), custom_call_target="tpu_custom_call" | custom-call | flops 6000000000 | tf_op jit(solution)/shard_map/combine/pallas_call | solution.py:135
  71.6 13.3 %collective-permute-start.19 = (f32[16,5,16,128]{3,2,1,0:T(8,128)}, f32[16,5,16,128]{3,2,1,0:T(8,128)S(1)}, u32[]{:S(2)}, u32[]{:S(2)}) collective-permute-start(f32[16,5,16,128]{3,2,1,0:T(8,128)} %collective-permute-done.18.refs_1_), channel_id=1, source_target_pairs={{0,2},{1,3},{6,4},{7,5},{8,10},{9,11},{14,12},{15,13},{16,18},{17,... | collective-permute-start | bytes 1966088 | tf_op jit(solution)/shard_map/ppermute | solution.py:350
  87.1 6.7 %collective-permute-done.10.refs_2_ = f32[16,5,8,128]{3,2,1,0:T(8,128)S(1)} collective-permute-done((f32[16,5,8,128]{3,2,1,0:T(8,128)S(1)}, f32[16,5,8,128]{3,2,1,0:T(8,128)S(1)}, u32[]{:S(2)}, u32[]{:S(2)}) %collective-permute-start.10) | collective-permute-done | bytes 327712 | tf_op jit(solution)/shard_map/ppermute | solution.py:350
  93.9 1.3 collective-permute-start.13
  95.2 1.5 collective-permute-start.23
  96.7 6.6 %collective-permute-done.13.refs_1_.refs_5_ = f32[8,5,8,128]{3,2,1,0:T(8,128)S(1)} collective-permute-done((f32[8,5,8,128]{3,2,1,0:T(8,128)S(1)}, f32[8,5,8,128]{3,2,1,0:T(8,128)S(1)}, u32[]{:S(2)}, u32[]{:S(2)}) %collective-permute-start.13) | collective-permute-done | bytes 163872 | tf_op jit(solution)/shard_map/ppermute | solution.py:358
  104.2 2.0 combine.7
  107.7 4.6 %collective-permute-start.24 = (f32[16,5,16,128]{3,2,1,0:T(8,128)S(1)}, f32[16,5,16,128]{3,2,1,0:T(8,128)S(1)}, u32[]{:S(2)}, u32[]{:S(2)}) collective-permute-start(f32[16,5,16,128]{3,2,1,0:T(8,128)S(1)} %collective-permute-done.22.refs_1_), channel_id=1, source_target_pairs={{0,2},{1,3},{6,4},{7,5},{8,10},{9,11},{14,12},{15,13},{16,18},{17,... | collective-permute-start | bytes 1966088 | tf_op jit(solution)/shard_map/ppermute | solution.py:350
  113.1 2.2 collective-permute-start.30
  115.4 5.7 %collective-permute-done.20.refs_2_ = f32[16,5,16,128]{3,2,1,0:T(8,128)S(1)} collective-permute-done((f32[16,5,16,128]{3,2,1,0:T(8,128)S(1)}, f32[16,5,16,128]{3,2,1,0:T(8,128)S(1)}, u32[]{:S(2)}, u32[]{:S(2)}) %collective-permute-start.20) | collective-permute-done | bytes 655392 | tf_op jit(solution)/shard_map/ppermute | solution.py:350
  121.1 2.6 %collective-permute-done.24.refs_3_ = f32[16,5,16,128]{3,2,1,0:T(8,128)S(1)} collective-permute-done((f32[16,5,16,128]{3,2,1,0:T(8,128)S(1)}, f32[16,5,16,128]{3,2,1,0:T(8,128)S(1)}, u32[]{:S(2)}, u32[]{:S(2)}) %collective-permute-start.24) | collective-permute-done | bytes 655392 | tf_op jit(solution)/shard_map/ppermute | solution.py:350
  123.8 2.6 %collective-permute-start.21 = (f32[8,5,16,128]{3,2,1,0:T(8,128)S(1)}, f32[8,5,16,128]{3,2,1,0:T(8,128)S(1)}, u32[]{:S(2)}, u32[]{:S(2)}) collective-permute-start(f32[8,5,16,128]{3,2,1,0:T(8,128)S(1)} %get-tuple-element.244), channel_id=1, source_target_pairs={{0,1},{1,0},{2,3},{3,2},{4,5},{5,4},{6,7},{7,6},{8,9},{9,8},{10,11... | collective-permute-start | bytes 983048 | tf_op jit(solution)/shard_map/ppermute | solution.py:358
  128.4 11.5 %collective-permute-start.32 = (f32[16,5,8,128]{3,2,1,0:T(8,128)S(1)}, f32[16,5,8,128]{3,2,1,0:T(8,128)S(1)}, u32[]{:S(2)}, u32[]{:S(2)}) collective-permute-start(f32[16,5,8,128]{3,2,1,0:T(8,128)S(1)} %collective-permute-done.30.refs_1_), channel_id=1, source_target_pairs={{0,2},{1,3},{6,4},{7,5},{8,10},{9,11},{14,12},{15,13},{16,18},{17,... | collective-permute-start | bytes 983048 | tf_op jit(solution)/shard_map/ppermute | solution.py:350
  140.0 1.3 collective-permute-start.31
  143.8 4.3 %collective-permute-done.32.refs_3_ = f32[16,5,8,128]{3,2,1,0:T(8,128)S(1)} collective-permute-done((f32[16,5,8,128]{3,2,1,0:T(8,128)S(1)}, f32[16,5,8,128]{3,2,1,0:T(8,128)S(1)}, u32[]{:S(2)}, u32[]{:S(2)}) %collective-permute-start.32) | collective-permute-done | bytes 327712 | tf_op jit(solution)/shard_map/ppermute | solution.py:350
  148.9 5.1 %collective-permute-done.31.refs_2_ = f32[16,5,8,128]{3,2,1,0:T(8,128)S(1)} collective-permute-done((f32[16,5,8,128]{3,2,1,0:T(8,128)S(1)}, f32[16,5,8,128]{3,2,1,0:T(8,128)S(1)}, u32[]{:S(2)}, u32[]{:S(2)}) %collective-permute-start.31) | collective-permute-done | bytes 327712 | tf_op jit(solution)/shard_map/ppermute | solution.py:350
  155.0 5.5 %collective-permute-done.29.refs_2_ = f32[16,5,16,128]{3,2,1,0:T(8,128)S(1)} collective-permute-done((f32[16,5,16,128]{3,2,1,0:T(8,128)S(1)}, f32[16,5,16,128]{3,2,1,0:T(8,128)S(1)}, u32[]{:S(2)}, u32[]{:S(2)}) %collective-permute-start.29) | collective-permute-done | bytes 655392 | tf_op jit(solution)/shard_map/ppermute | solution.py:350
  161.7 7.3 %collective-permute-done.33.refs_1_.refs_7_ = f32[8,5,16,128]{3,2,1,0:T(8,128)S(1)} collective-permute-done((f32[8,5,16,128]{3,2,1,0:T(8,128)S(1)}, f32[8,5,16,128]{3,2,1,0:T(8,128)S(1)}, u32[]{:S(2)}, u32[]{:S(2)}) %collective-permute-start.33) | collective-permute-done | bytes 327712 | tf_op jit(solution)/shard_map/ppermute | solution.py:358
  172.9 1.7 collective-permute-start.36
  174.6 14.6 %collective-permute-done.38.refs_2_ = f32[16,5,16,128]{3,2,1,0:T(8,128)S(1)} collective-permute-done((f32[16,5,16,128]{3,2,1,0:T(8,128)S(1)}, f32[16,5,16,128]{3,2,1,0:T(8,128)S(1)}, u32[]{:S(2)}, u32[]{:S(2)}) %collective-permute-start.38) | collective-permute-done | bytes 655392 | tf_op jit(solution)/shard_map/ppermute | solution.py:350
  189.4 4.1 %collective-permute-done.41.refs_2_ = f32[16,5,8,128]{3,2,1,0:T(8,128)S(1)} collective-permute-done((f32[16,5,8,128]{3,2,1,0:T(8,128)S(1)}, f32[16,5,8,128]{3,2,1,0:T(8,128)S(1)}, u32[]{:S(2)}, u32[]{:S(2)}) %collective-permute-start.41) | collective-permute-done | bytes 327712 | tf_op jit(solution)/shard_map/ppermute | solution.py:350
  193.5 2.9 %collective-permute-done.40.refs_1_.refs_8_ = f32[8,5,16,128]{3,2,1,0:T(8,128)S(1)} collective-permute-done((f32[8,5,16,128]{3,2,1,0:T(8,128)S(1)}, f32[8,5,16,128]{3,2,1,0:T(8,128)S(1)}, u32[]{:S(2)}, u32[]{:S(2)}) %collective-permute-start.40) | collective-permute-done | bytes 327712 | tf_op jit(solution)/shard_map/ppermute | solution.py:358
  197.5 1.7 collective-permute-start.44
  199.2 6.2 %collective-permute-done.45.refs_9_.refs_1_ = f32[8,5,8,128]{3,2,1,0:T(8,128)S(1)} collective-permute-done((f32[8,5,8,128]{3,2,1,0:T(8,128)S(1)}, f32[8,5,8,128]{3,2,1,0:T(8,128)S(1)}, u32[]{:S(2)}, u32[]{:S(2)}) %collective-permute-start.45) | collective-permute-done | bytes 163872 | tf_op jit(solution)/shard_map/ppermute | solution.py:358
  205.4 1.4 collective-permute-done.42.refs_13_
  208.0 1.5 collective-permute-done.44.refs_15_
  210.4 4.8 %collective-permute-start.46 = (f32[4,5,16,128]{3,2,1,0:T(8,128)S(1)}, f32[4,5,16,128]{3,2,1,0:T(8,128)S(1)}, u32[]{:S(2)}, u32[]{:S(2)}) collective-permute-start(f32[4,5,16,128]{3,2,1,0:T(8,128)S(1)} %get-tuple-element.339), channel_id=1, source_target_pairs={{0,8},{8,16},{16,24},{24,0},{1,9},{9,17},{17,25},{25,1},{2,10},{10... | collective-permute-start | bytes 491528 | tf_op jit(solution)/shard_map/ppermute | solution.py:466
  215.2 1.4 collective-permute-start.48
  216.6 3.1 %place_one.1 = f32[8,5,128,128]{3,2,1,0:T(8,128)} custom-call(s32[1]{0:T(128)} %bitcast.place_ref, f32[8,5,8,128]{3,2,1,0:T(8,128)S(1)} %get-tuple-element.221.refs_0_, f32[8,5,16,128]{3,2,1,0:T(8,128)S(1)} %get-tuple-element.256.refs_0_.refs_1_, f32[8,5,16,128]{3,2,1,0:T(8,128)S(1)} %get-tuple-element.282.refs_0_.refs_2_, ...), custom_call_target="tpu_custom_call" | custom-call | bytes 5242880 | tf_op jit(solution)/shard_map/place_one/pallas_call | solution.py:219
  219.7 1.6 collective-permute-done.47.refs_18_
  222.6 2.6 %last.1 = f32[4,5,128,128]{3,2,1,0:T(8,128)} custom-call(s32[1]{0:T(128)} %bitcast.place_ref, f32[128,128]{1,0:T(8,128)S(1)} %copy-done.2, f32[4,5,16,128]{3,2,1,0:T(8,128)S(1)} %get-tuple-element.320.refs_0_, f32[4,5,16,128]{3,2,1,0:T(8,128)S(1)} %collective-permute-done.14.refs_1_, f32[4,5,16,128]{3,2,1,0:T(8,128)S(1)} %collective-permute-done.15.refs_2_, ...), custom_call_target="tpu_custom_call" | custom-call | flops 671088640 | bytes 6553600 | tf_op jit(solution)/shard_map/last/pallas_call | solution.py:266
  (116 shorter events, 29.7 us)
Async XLA Ops:
  0.6 10.8 %collective-permute-start.1 = (f32[16,128]{1,0:T(8,128)}, f32[16,128]{1,0:T(8,128)S(1)}, u32[]{:S(2)}, u32[]{:S(2)}) collective-permute-start(f32[16,128]{1,0:T(8,128)} %param.21), channel_id=1, source_target_pairs={{0,1},{1,2},{2,3},{3,4},{4,5},{5,6},{6,7},{7,8},{8,9},{9,10},{10,1... | collective-permute-start | bytes 24584 | tf_op jit(solution)/shard_map/ppermute | solution.py:297
  3.6 7.8 %collective-permute-start.2 = (f32[16,128]{1,0:T(8,128)}, f32[16,128]{1,0:T(8,128)S(1)}, u32[]{:S(2)}, u32[]{:S(2)}) collective-permute-start(f32[16,128]{1,0:T(8,128)} %param.21), channel_id=1, source_target_pairs={{0,31},{1,0},{2,1},{3,2},{4,3},{5,4},{6,5},{7,6},{8,7},{9,8},{10,9... | collective-permute-start | bytes 24584 | tf_op jit(solution)/shard_map/ppermute | solution.py:298
  22.7 8.2 %collective-permute-start.7 = (f32[16,5,8,128]{3,2,1,0:T(8,128)S(1)}, f32[16,5,8,128]{3,2,1,0:T(8,128)S(1)}, u32[]{:S(2)}, u32[]{:S(2)}) collective-permute-start(f32[16,5,8,128]{3,2,1,0:T(8,128)S(1)} %get-tuple-element.182), channel_id=1, source_target_pairs={{0,1},{1,0},{2,3},{3,2},{4,5},{5,4},{6,7},{7,6},{8,9},{9,8},{10,11... | collective-permute-start | bytes 983048 | tf_op jit(solution)/shard_map/ppermute | solution.py:358
  22.7 14.7 %collective-permute-start.3 = (f32[16,5,8,128]{3,2,1,0:T(8,128)S(1)}, f32[16,5,8,128]{3,2,1,0:T(8,128)S(1)}, u32[]{:S(2)}, u32[]{:S(2)}) collective-permute-start(f32[16,5,8,128]{3,2,1,0:T(8,128)S(1)} %get-tuple-element.184.refs_0_), channel_id=1, source_target_pairs={{0,2},{1,3},{6,4},{7,5},{8,10},{9,11},{14,12},{15,13},{16,18},{17,... | collective-permute-start | bytes 983048 | tf_op jit(solution)/shard_map/ppermute | solution.py:350
  30.9 12.0 %collective-permute-start.8 = (f32[16,5,8,128]{3,2,1,0:T(8,128)S(1)}, f32[16,5,8,128]{3,2,1,0:T(8,128)S(1)}, u32[]{:S(2)}, u32[]{:S(2)}) collective-permute-start(f32[16,5,8,128]{3,2,1,0:T(8,128)S(1)} %collective-permute-done.7.refs_1_), channel_id=1, source_target_pairs={{0,2},{1,3},{6,4},{7,5},{8,10},{9,11},{14,12},{15,13},{16,18},{17,... | collective-permute-start | bytes 983048 | tf_op jit(solution)/shard_map/ppermute | solution.py:350
  32.2 5.2 %collective-permute-start.4 = (s32[2,16]{1,0:T(2,128)S(1)}, s32[2,16]{1,0:T(2,128)S(1)}, u32[]{:S(2)}, u32[]{:S(2)}) collective-permute-start(s32[2,16]{1,0:T(2,128)S(1)} %pad_add_fusion.1), channel_id=1, source_target_pairs={{0,2},{1,3},{6,4},{7,5},{8,10},{9,11},{14,12},{15,13},{16,18},{17,... | collective-permute-start | bytes 392 | tf_op jit(solution)/shard_map/ppermute | solution.py:350
  33.5 16.9 %collective-permute-start.11 = (f32[16,5,16,128]{3,2,1,0:T(8,128)}, f32[16,5,16,128]{3,2,1,0:T(8,128)}, u32[]{:S(2)}, u32[]{:S(2)}) collective-permute-start(f32[16,5,16,128]{3,2,1,0:T(8,128)} %get-tuple-element.199), channel_id=1, source_target_pairs={{0,1},{1,0},{2,3},{3,2},{4,5},{5,4},{6,7},{7,6},{8,9},{9,8},{10,11... | collective-permute-start | bytes 1966088 | tf_op jit(solution)/shard_map/ppermute | solution.py:358
  37.4 16.9 %collective-permute-start.5 = (f32[16,5,16,128]{3,2,1,0:T(8,128)}, f32[16,5,16,128]{3,2,1,0:T(8,128)}, u32[]{:S(2)}, u32[]{:S(2)}) collective-permute-start(f32[16,5,16,128]{3,2,1,0:T(8,128)} %get-tuple-element.209.refs_0_), channel_id=1, source_target_pairs={{0,2},{1,3},{6,4},{7,5},{8,10},{9,11},{14,12},{15,13},{16,18},{17,... | collective-permute-start | bytes 1966088 | tf_op jit(solution)/shard_map/ppermute | solution.py:350
  44.7 14.8 %collective-permute-start.9 = (f32[32,5,8,128]{3,2,1,0:T(8,128)}, f32[32,5,8,128]{3,2,1,0:T(8,128)S(1)}, u32[]{:S(2)}, u32[]{:S(2)}) collective-permute-start(f32[32,5,8,128]{3,2,1,0:T(8,128)} %get-tuple-element.189), channel_id=1, source_target_pairs={{2,4},{3,5},{4,2},{5,3},{10,12},{11,13},{12,10},{13,11},{18,20},{1... | collective-permute-start | bytes 1966088 | tf_op jit(solution)/shard_map/ppermute | solution.py:426
  45.6 26.0 %collective-permute-start.18 = (f32[16,5,16,128]{3,2,1,0:T(8,128)}, f32[16,5,16,128]{3,2,1,0:T(8,128)}, u32[]{:S(2)}, u32[]{:S(2)}) collective-permute-start(f32[16,5,16,128]{3,2,1,0:T(8,128)} %get-tuple-element.228), channel_id=1, source_target_pairs={{0,1},{1,0},{2,3},{3,2},{4,5},{5,4},{6,7},{7,6},{8,9},{9,8},{10,11... | collective-permute-start | bytes 1966088 | tf_op jit(solution)/shard_map/ppermute | solution.py:358
  50.4 18.0 %collective-permute-start.12 = (f32[16,5,16,128]{3,2,1,0:T(8,128)}, f32[16,5,16,128]{3,2,1,0:T(8,128)}, u32[]{:S(2)}, u32[]{:S(2)}) collective-permute-start(f32[16,5,16,128]{3,2,1,0:T(8,128)} %collective-permute-done.11.refs_1_), channel_id=1, source_target_pairs={{0,2},{1,3},{6,4},{7,5},{8,10},{9,11},{14,12},{15,13},{16,18},{17,... | collective-permute-start | bytes 1966088 | tf_op jit(solution)/shard_map/ppermute | solution.py:350
  54.3 32.8 %collective-permute-start.6 = (f32[16,5,16,128]{3,2,1,0:T(8,128)S(1)}, f32[16,5,16,128]{3,2,1,0:T(8,128)}, u32[]{:S(2)}, u32[]{:S(2)}) collective-permute-start(f32[16,5,16,128]{3,2,1,0:T(8,128)S(1)} %copy-done.4), channel_id=1, source_target_pairs={{0,2},{1,3},{6,4},{7,5},{8,10},{9,11},{14,12},{15,13},{16,18},{17,... | collective-permute-start | bytes 1966088 | tf_op jit(solution)/shard_map/ppermute | solution.py:350
  70.8 35.4 %collective-permute-start.17 = (f32[32,5,16,128]{3,2,1,0:T(8,128)S(1)}, f32[32,5,16,128]{3,2,1,0:T(8,128)S(1)}, u32[]{:S(2)}, u32[]{:S(2)}) collective-permute-start(f32[32,5,16,128]{3,2,1,0:T(8,128)S(1)} %get-tuple-element.213), channel_id=1, source_target_pairs={{2,4},{3,5},{4,2},{5,3},{10,12},{11,13},{12,10},{13,11},{18,20},{1... | collective-permute-start | bytes 3932168 | tf_op jit(solution)/shard_map/ppermute | solution.py:426
  71.6 32.6 %collective-permute-start.19 = (f32[16,5,16,128]{3,2,1,0:T(8,128)}, f32[16,5,16,128]{3,2,1,0:T(8,128)S(1)}, u32[]{:S(2)}, u32[]{:S(2)}) collective-permute-start(f32[16,5,16,128]{3,2,1,0:T(8,128)} %collective-permute-done.18.refs_1_), channel_id=1, source_target_pairs={{0,2},{1,3},{6,4},{7,5},{8,10},{9,11},{14,12},{15,13},{16,18},{17,... | collective-permute-start | bytes 1966088 | tf_op jit(solution)/shard_map/ppermute | solution.py:350
  84.8 9.0 %collective-permute-start.10 = (f32[16,5,8,128]{3,2,1,0:T(8,128)S(1)}, f32[16,5,8,128]{3,2,1,0:T(8,128)S(1)}, u32[]{:S(2)}, u32[]{:S(2)}) collective-permute-start(f32[16,5,8,128]{3,2,1,0:T(8,128)S(1)} %get-tuple-element.194), channel_id=1, source_target_pairs={{2,0},{3,1},{4,6},{5,7},{10,8},{11,9},{12,14},{13,15},{18,16},{19,... | collective-permute-start | bytes 983048 | tf_op jit(solution)/shard_map/ppermute | solution.py:350
  86.2 21.6 %collective-permute-start.22 = (f32[16,5,16,128]{3,2,1,0:T(8,128)S(1)}, f32[16,5,16,128]{3,2,1,0:T(8,128)S(1)}, u32[]{:S(2)}, u32[]{:S(2)}) collective-permute-start(f32[16,5,16,128]{3,2,1,0:T(8,128)S(1)} %copy-done.11), channel_id=1, source_target_pairs={{0,1},{1,0},{2,3},{3,2},{4,5},{5,4},{6,7},{7,6},{8,9},{9,8},{10,11... | collective-permute-start | bytes 1966088 | tf_op jit(solution)/shard_map/ppermute | solution.py:358
  93.9 9.5 %collective-permute-start.13 = (f32[8,5,8,128]{3,2,1,0:T(8,128)S(1)}, f32[8,5,8,128]{3,2,1,0:T(8,128)S(1)}, u32[]{:S(2)}, u32[]{:S(2)}) collective-permute-start(f32[8,5,8,128]{3,2,1,0:T(8,128)S(1)} %get-tuple-element.218), channel_id=1, source_target_pairs={{0,1},{1,0},{2,3},{3,2},{4,5},{5,4},{6,7},{7,6},{8,9},{9,8},{10,11... | collective-permute-start | bytes 491528 | tf_op jit(solution)/shard_map/ppermute | solution.py:358
  95.2 20.1 %collective-permute-start.23 = (f32[16,5,16,128]{3,2,1,0:T(8,128)S(1)}, f32[16,5,16,128]{3,2,1,0:T(8,128)S(1)}, u32[]{:S(2)}, u32[]{:S(2)}) collective-permute-start(f32[16,5,16,128]{3,2,1,0:T(8,128)S(1)} %copy-done.3), channel_id=1, source_target_pairs={{0,2},{1,3},{6,4},{7,5},{8,10},{9,11},{14,12},{15,13},{16,18},{17,... | collective-permute-start | bytes 1966088 | tf_op jit(solution)/shard_map/ppermute | solution.py:350
  106.4 14.7 %collective-permute-start.20 = (f32[16,5,16,128]{3,2,1,0:T(8,128)S(1)}, f32[16,5,16,128]{3,2,1,0:T(8,128)S(1)}, u32[]{:S(2)}, u32[]{:S(2)}) collective-permute-start(f32[16,5,16,128]{3,2,1,0:T(8,128)S(1)} %get-tuple-element.239), channel_id=1, source_target_pairs={{2,0},{3,1},{4,6},{5,7},{10,8},{11,9},{12,14},{13,15},{18,16},{19,... | collective-permute-start | bytes 1966088 | tf_op jit(solution)/shard_map/ppermute | solution.py:350
  107.7 16.0 %collective-permute-start.24 = (f32[16,5,16,128]{3,2,1,0:T(8,128)S(1)}, f32[16,5,16,128]{3,2,1,0:T(8,128)S(1)}, u32[]{:S(2)}, u32[]{:S(2)}) collective-permute-start(f32[16,5,16,128]{3,2,1,0:T(8,128)S(1)} %collective-permute-done.22.refs_1_), channel_id=1, source_target_pairs={{0,2},{1,3},{6,4},{7,5},{8,10},{9,11},{14,12},{15,13},{16,18},{17,... | collective-permute-start | bytes 1966088 | tf_op jit(solution)/shard_map/ppermute | solution.py:350
  112.4 29.9 %collective-permute-start.28 = (f32[32,5,16,128]{3,2,1,0:T(8,128)S(1)}, f32[32,5,16,128]{3,2,1,0:T(8,128)S(1)}, u32[]{:S(2)}, u32[]{:S(2)}) collective-permute-start(f32[32,5,16,128]{3,2,1,0:T(8,128)S(1)} %get-tuple-element.234), channel_id=1, source_target_pairs={{2,4},{3,5},{4,2},{5,3},{10,12},{11,13},{12,10},{13,11},{18,20},{1... | collective-permute-start | bytes 3932168 | tf_op jit(solution)/shard_map/ppermute | solution.py:426
  113.1 10.6 %collective-permute-start.30 = (f32[16,5,8,128]{3,2,1,0:T(8,128)S(1)}, f32[16,5,8,128]{3,2,1,0:T(8,128)S(1)}, u32[]{:S(2)}, u32[]{:S(2)}) collective-permute-start(f32[16,5,8,128]{3,2,1,0:T(8,128)S(1)} %copy-done.12), channel_id=1, source_target_pairs={{0,1},{1,0},{2,3},{3,2},{4,5},{5,4},{6,7},{7,6},{8,9},{9,8},{10,11... | collective-permute-start | bytes 983048 | tf_op jit(solution)/shard_map/ppermute | solution.py:358
  115.3 12.3 %collective-permute-start.14 = (f32[4,5,16,128]{3,2,1,0:T(8,128)S(1)}, f32[4,5,16,128]{3,2,1,0:T(8,128)S(1)}, u32[]{:S(2)}, u32[]{:S(2)}) collective-permute-start(f32[4,5,16,128]{3,2,1,0:T(8,128)S(1)} %get-tuple-element.224), channel_id=1, source_target_pairs={{0,8},{8,16},{16,24},{24,0},{1,9},{9,17},{17,25},{25,1},{2,10},{10... | collective-permute-start | bytes 491528 | tf_op jit(solution)/shard_map/ppermute | solution.py:466
  121.1 7.4 %collective-permute-start.15 = (f32[4,5,16,128]{3,2,1,0:T(8,128)S(1)}, f32[4,5,16,128]{3,2,1,0:T(8,128)S(1)}, u32[]{:S(2)}, u32[]{:S(2)}) collective-permute-start(f32[4,5,16,128]{3,2,1,0:T(8,128)S(1)} %get-tuple-element.225), channel_id=1, source_target_pairs={{0,16},{8,24},{16,0},{24,8},{1,17},{9,25},{17,1},{25,9},{2,18},{10... | collective-permute-start | bytes 491528 | tf_op jit(solution)/shard_map/ppermute | solution.py:466
  123.7 16.2 %collective-permute-start.16 = (f32[4,5,16,128]{3,2,1,0:T(8,128)S(1)}, f32[4,5,16,128]{3,2,1,0:T(8,128)S(1)}, u32[]{:S(2)}, u32[]{:S(2)}) collective-permute-start(f32[4,5,16,128]{3,2,1,0:T(8,128)S(1)} %get-tuple-element.226), channel_id=1, source_target_pairs={{0,24},{8,0},{16,8},{24,16},{1,25},{9,1},{17,9},{25,17},{2,26},{10... | collective-permute-start | bytes 491528 | tf_op jit(solution)/shard_map/ppermute | solution.py:466
  123.8 17.5 %collective-permute-start.21 = (f32[8,5,16,128]{3,2,1,0:T(8,128)S(1)}, f32[8,5,16,128]{3,2,1,0:T(8,128)S(1)}, u32[]{:S(2)}, u32[]{:S(2)}) collective-permute-start(f32[8,5,16,128]{3,2,1,0:T(8,128)S(1)} %get-tuple-element.244), channel_id=1, source_target_pairs={{0,1},{1,0},{2,3},{3,2},{4,5},{5,4},{6,7},{7,6},{8,9},{9,8},{10,11... | collective-permute-start | bytes 983048 | tf_op jit(solution)/shard_map/ppermute | solution.py:358
  127.7 42.2 %collective-permute-start.37 = (f32[32,5,16,128]{3,2,1,0:T(8,128)S(1)}, f32[32,5,16,128]{3,2,1,0:T(8,128)S(1)}, u32[]{:S(2)}, u32[]{:S(2)}) collective-permute-start(f32[32,5,16,128]{3,2,1,0:T(8,128)S(1)} %get-tuple-element.255), channel_id=1, source_target_pairs={{2,4},{3,5},{4,2},{5,3},{10,12},{11,13},{12,10},{13,11},{18,20},{1... | collective-permute-start | bytes 3932168 | tf_op jit(solution)/shard_map/ppermute | solution.py:426
  128.4 19.6 %collective-permute-start.32 = (f32[16,5,8,128]{3,2,1,0:T(8,128)S(1)}, f32[16,5,8,128]{3,2,1,0:T(8,128)S(1)}, u32[]{:S(2)}, u32[]{:S(2)}) collective-permute-start(f32[16,5,8,128]{3,2,1,0:T(8,128)S(1)} %collective-permute-done.30.refs_1_), channel_id=1, source_target_pairs={{0,2},{1,3},{6,4},{7,5},{8,10},{9,11},{14,12},{15,13},{16,18},{17,... | collective-permute-start | bytes 983048 | tf_op jit(solution)/shard_map/ppermute | solution.py:350
  140.0 14.0 %collective-permute-start.31 = (f32[16,5,8,128]{3,2,1,0:T(8,128)S(1)}, f32[16,5,8,128]{3,2,1,0:T(8,128)S(1)}, u32[]{:S(2)}, u32[]{:S(2)}) collective-permute-start(f32[16,5,8,128]{3,2,1,0:T(8,128)S(1)} %copy-done.5), channel_id=1, source_target_pairs={{0,2},{1,3},{6,4},{7,5},{8,10},{9,11},{14,12},{15,13},{16,18},{17,... | collective-permute-start | bytes 983048 | tf_op jit(solution)/shard_map/ppermute | solution.py:350
  142.4 18.1 %collective-permute-start.29 = (f32[16,5,16,128]{3,2,1,0:T(8,128)S(1)}, f32[16,5,16,128]{3,2,1,0:T(8,128)S(1)}, u32[]{:S(2)}, u32[]{:S(2)}) collective-permute-start(f32[16,5,16,128]{3,2,1,0:T(8,128)S(1)} %get-tuple-element.267), channel_id=1, source_target_pairs={{2,0},{3,1},{4,6},{5,7},{10,8},{11,9},{12,14},{13,15},{18,16},{19,... | collective-permute-start | bytes 1966088 | tf_op jit(solution)/shard_map/ppermute | solution.py:350
  143.7 17.3 %collective-permute-start.25 = (f32[4,5,32,128]{3,2,1,0:T(8,128)S(1)}, f32[4,5,32,128]{3,2,1,0:T(8,128)S(1)}, u32[]{:S(2)}, u32[]{:S(2)}) collective-permute-start(f32[4,5,32,128]{3,2,1,0:T(8,128)S(1)} %get-tuple-element.259), channel_id=1, source_target_pairs={{0,8},{8,16},{16,24},{24,0},{1,9},{9,17},{17,25},{25,1},{2,10},{10... | collective-permute-start | bytes 983048 | tf_op jit(solution)/shard_map/ppermute | solution.py:466
  148.0 13.6 %collective-permute-start.26 = (f32[4,5,32,128]{3,2,1,0:T(8,128)S(1)}, f32[4,5,32,128]{3,2,1,0:T(8,128)S(1)}, u32[]{:S(2)}, u32[]{:S(2)}) collective-permute-start(f32[4,5,32,128]{3,2,1,0:T(8,128)S(1)} %get-tuple-element.260), channel_id=1, source_target_pairs={{0,16},{8,24},{16,0},{24,8},{1,17},{9,25},{17,1},{25,9},{2,18},{10... | collective-permute-start | bytes 983048 | tf_op jit(solution)/shard_map/ppermute | solution.py:466
  153.9 7.7 %collective-permute-start.27 = (f32[4,5,32,128]{3,2,1,0:T(8,128)S(1)}, f32[4,5,32,128]{3,2,1,0:T(8,128)S(1)}, u32[]{:S(2)}, u32[]{:S(2)}) collective-permute-start(f32[4,5,32,128]{3,2,1,0:T(8,128)S(1)} %get-tuple-element.261), channel_id=1, source_target_pairs={{0,24},{8,0},{16,8},{24,16},{1,25},{9,1},{17,9},{25,17},{2,26},{10... | collective-permute-start | bytes 983048 | tf_op jit(solution)/shard_map/ppermute | solution.py:466
  160.6 8.4 %collective-permute-start.33 = (f32[8,5,16,128]{3,2,1,0:T(8,128)S(1)}, f32[8,5,16,128]{3,2,1,0:T(8,128)S(1)}, u32[]{:S(2)}, u32[]{:S(2)}) collective-permute-start(f32[8,5,16,128]{3,2,1,0:T(8,128)S(1)} %get-tuple-element.279), channel_id=1, source_target_pairs={{0,1},{1,0},{2,3},{3,2},{4,5},{5,4},{6,7},{7,6},{8,9},{9,8},{10,11... | collective-permute-start | bytes 983048 | tf_op jit(solution)/shard_map/ppermute | solution.py:358
  161.0 10.6 %collective-permute-start.39 = (f32[32,5,8,128]{3,2,1,0:T(8,128)S(1)}, f32[32,5,8,128]{3,2,1,0:T(8,128)S(1)}, u32[]{:S(2)}, u32[]{:S(2)}) collective-permute-start(f32[32,5,8,128]{3,2,1,0:T(8,128)S(1)} %get-tuple-element.274), channel_id=1, source_target_pairs={{2,4},{3,5},{4,2},{5,3},{10,12},{11,13},{12,10},{13,11},{18,20},{1... | collective-permute-start | bytes 1966088 | tf_op jit(solution)/shard_map/ppermute | solution.py:426
  170.1 19.1 %collective-permute-start.38 = (f32[16,5,16,128]{3,2,1,0:T(8,128)S(1)}, f32[16,5,16,128]{3,2,1,0:T(8,128)S(1)}, u32[]{:S(2)}, u32[]{:S(2)}) collective-permute-start(f32[16,5,16,128]{3,2,1,0:T(8,128)S(1)} %get-tuple-element.293), channel_id=1, source_target_pairs={{2,0},{3,1},{4,6},{5,7},{10,8},{11,9},{12,14},{13,15},{18,16},{19,... | collective-permute-start | bytes 1966088 | tf_op jit(solution)/shard_map/ppermute | solution.py:350
  171.4 22.1 %collective-permute-start.34 = (f32[4,5,32,128]{3,2,1,0:T(8,128)S(1)}, f32[4,5,32,128]{3,2,1,0:T(8,128)S(1)}, u32[]{:S(2)}, u32[]{:S(2)}) collective-permute-start(f32[4,5,32,128]{3,2,1,0:T(8,128)S(1)} %get-tuple-element.285), channel_id=1, source_target_pairs={{0,8},{8,16},{16,24},{24,0},{1,9},{9,17},{17,25},{25,1},{2,10},{10... | collective-permute-start | bytes 983048 | tf_op jit(solution)/shard_map/ppermute | solution.py:466
  171.5 22.0 %collective-permute-start.35 = (f32[4,5,32,128]{3,2,1,0:T(8,128)S(1)}, f32[4,5,32,128]{3,2,1,0:T(8,128)S(1)}, u32[]{:S(2)}, u32[]{:S(2)}) collective-permute-start(f32[4,5,32,128]{3,2,1,0:T(8,128)S(1)} %get-tuple-element.286), channel_id=1, source_target_pairs={{0,16},{8,24},{16,0},{24,8},{1,17},{9,25},{17,1},{25,9},{2,18},{10... | collective-permute-start | bytes 983048 | tf_op jit(solution)/shard_map/ppermute | solution.py:466
  171.6 21.8 %collective-permute-start.41 = (f32[16,5,8,128]{3,2,1,0:T(8,128)S(1)}, f32[16,5,8,128]{3,2,1,0:T(8,128)S(1)}, u32[]{:S(2)}, u32[]{:S(2)}) collective-permute-start(f32[16,5,8,128]{3,2,1,0:T(8,128)S(1)} %get-tuple-element.297), channel_id=1, source_target_pairs={{2,0},{3,1},{4,6},{5,7},{10,8},{11,9},{12,14},{13,15},{18,16},{19,... | collective-permute-start | bytes 983048 | tf_op jit(solution)/shard_map/ppermute | solution.py:350
  172.9 20.6 %collective-permute-start.36 = (f32[4,5,32,128]{3,2,1,0:T(8,128)S(1)}, f32[4,5,32,128]{3,2,1,0:T(8,128)S(1)}, u32[]{:S(2)}, u32[]{:S(2)}) collective-permute-start(f32[4,5,32,128]{3,2,1,0:T(8,128)S(1)} %get-tuple-element.287), channel_id=1, source_target_pairs={{0,24},{8,0},{16,8},{24,16},{1,25},{9,1},{17,9},{25,17},{2,26},{10... | collective-permute-start | bytes 983048 | tf_op jit(solution)/shard_map/ppermute | solution.py:466
  189.3 7.1 %collective-permute-start.40 = (f32[8,5,16,128]{3,2,1,0:T(8,128)S(1)}, f32[8,5,16,128]{3,2,1,0:T(8,128)S(1)}, u32[]{:S(2)}, u32[]{:S(2)}) collective-permute-start(f32[8,5,16,128]{3,2,1,0:T(8,128)S(1)} %get-tuple-element.302), channel_id=1, source_target_pairs={{0,1},{1,0},{2,3},{3,2},{4,5},{5,4},{6,7},{7,6},{8,9},{9,8},{10,11... | collective-permute-start | bytes 983048 | tf_op jit(solution)/shard_map/ppermute | solution.py:358
  197.4 9.5 %collective-permute-start.42 = (f32[4,5,32,128]{3,2,1,0:T(8,128)S(1)}, f32[4,5,32,128]{3,2,1,0:T(8,128)S(1)}, u32[]{:S(2)}, u32[]{:S(2)}) collective-permute-start(f32[4,5,32,128]{3,2,1,0:T(8,128)S(1)} %get-tuple-element.314), channel_id=1, source_target_pairs={{0,8},{8,16},{16,24},{24,0},{1,9},{9,17},{17,25},{25,1},{2,10},{10... | collective-permute-start | bytes 983048 | tf_op jit(solution)/shard_map/ppermute | solution.py:466
  197.4 10.6 %collective-permute-start.43 = (f32[4,5,32,128]{3,2,1,0:T(8,128)S(1)}, f32[4,5,32,128]{3,2,1,0:T(8,128)S(1)}, u32[]{:S(2)}, u32[]{:S(2)}) collective-permute-start(f32[4,5,32,128]{3,2,1,0:T(8,128)S(1)} %get-tuple-element.315), channel_id=1, source_target_pairs={{0,16},{8,24},{16,0},{24,8},{1,17},{9,25},{17,1},{25,9},{2,18},{10... | collective-permute-start | bytes 983048 | tf_op jit(solution)/shard_map/ppermute | solution.py:466
  197.5 12.0 %collective-permute-start.44 = (f32[4,5,32,128]{3,2,1,0:T(8,128)S(1)}, f32[4,5,32,128]{3,2,1,0:T(8,128)S(1)}, u32[]{:S(2)}, u32[]{:S(2)}) collective-permute-start(f32[4,5,32,128]{3,2,1,0:T(8,128)S(1)} %get-tuple-element.316), channel_id=1, source_target_pairs={{0,24},{8,0},{16,8},{24,16},{1,25},{9,1},{17,9},{25,17},{2,26},{10... | collective-permute-start | bytes 983048 | tf_op jit(solution)/shard_map/ppermute | solution.py:466
  199.2 6.2 %collective-permute-start.45 = (f32[8,5,8,128]{3,2,1,0:T(8,128)S(1)}, f32[8,5,8,128]{3,2,1,0:T(8,128)S(1)}, u32[]{:S(2)}, u32[]{:S(2)}) collective-permute-start(f32[8,5,8,128]{3,2,1,0:T(8,128)S(1)} %get-tuple-element.317), channel_id=1, source_target_pairs={{0,1},{1,0},{2,3},{3,2},{4,5},{5,4},{6,7},{7,6},{8,9},{9,8},{10,11... | collective-permute-start | bytes 491528 | tf_op jit(solution)/shard_map/ppermute | solution.py:358
  210.4 9.3 %collective-permute-start.46 = (f32[4,5,16,128]{3,2,1,0:T(8,128)S(1)}, f32[4,5,16,128]{3,2,1,0:T(8,128)S(1)}, u32[]{:S(2)}, u32[]{:S(2)}) collective-permute-start(f32[4,5,16,128]{3,2,1,0:T(8,128)S(1)} %get-tuple-element.339), channel_id=1, source_target_pairs={{0,8},{8,16},{16,24},{24,0},{1,9},{9,17},{17,25},{25,1},{2,10},{10... | collective-permute-start | bytes 491528 | tf_op jit(solution)/shard_map/ppermute | solution.py:466
  215.2 6.2 %collective-permute-start.47 = (f32[4,5,16,128]{3,2,1,0:T(8,128)S(1)}, f32[4,5,16,128]{3,2,1,0:T(8,128)S(1)}, u32[]{:S(2)}, u32[]{:S(2)}) collective-permute-start(f32[4,5,16,128]{3,2,1,0:T(8,128)S(1)} %get-tuple-element.340), channel_id=1, source_target_pairs={{0,16},{8,24},{16,0},{24,8},{1,17},{9,25},{17,1},{25,9},{2,18},{10... | collective-permute-start | bytes 491528 | tf_op jit(solution)/shard_map/ppermute | solution.py:466
  215.2 7.4 %collective-permute-start.48 = (f32[4,5,16,128]{3,2,1,0:T(8,128)S(1)}, f32[4,5,16,128]{3,2,1,0:T(8,128)S(1)}, u32[]{:S(2)}, u32[]{:S(2)}) collective-permute-start(f32[4,5,16,128]{3,2,1,0:T(8,128)S(1)} %get-tuple-element.341), channel_id=1, source_target_pairs={{0,24},{8,0},{16,8},{24,16},{1,25},{9,1},{17,9},{25,17},{2,26},{10... | collective-permute-start | bytes 491528 | tf_op jit(solution)/shard_map/ppermute | solution.py:466
  (15 other events, 206.9 us)
where the time goes:
time: 226 us; the launch traced here: 225 us
  waiting for transfers between devices  99.4 us (44%)
  starting transfers between devices  88 us (39%)
  Pallas kernels  26.8 us (12%)
  local copies, waits for them, and re-layouts  4.93 us (2%)
  other arithmetic  4.73 us (2%)
    ppermute x16, starting transfers between devices, hop(): return lax.ppermute(array, 'member', pairs)  57.3 us
    ppermute x16, waiting for transfers between devices, hop(): return lax.ppermute(array, 'member', pairs)  56.1 us
    ppermute x11, waiting for transfers between devices, hop_x(): return lax.ppermute(array, 'member', pairs)  36.2 us
    pallas_call x20, Pallas kernels, whole(): pl.pallas_call(kernel, out_shape=out_shapes, in_specs=[pl.BlockSpec(memor...  14 us
    ppermute x15, starting transfers between devices, second(): received.append(lax.ppermute(share, 'group', circle) if way > 0 else share)  10.8 us
    ppermute x11, starting transfers between devices, hop_x(): return lax.ppermute(array, 'member', pairs)  9.76 us
    pallas_call x1, Pallas kernels, prepare(): pl.pallas_call(functools.partial(prepare_kernel, x_count), out_shape=[jax...  7.11 us
    ppermute x15, waiting for transfers between devices, second(): received.append(lax.ppermute(share, 'group', circle) if way > 0 else share)  7.04 us
  transfers between devices with their start and end apart: 49, of which 23 were waited for; matrix products, arithmetic and copies ran while one was open for 2% of the time, Pallas kernels for 7%

commit v1 on v0

--- a/solution.py
+++ b/solution.py
@@ -473,7 +473,7 @@
         time = swapped = max(rows_in, swapped) + step + pause
         turns += [(rows_in, 0, chunk), (time, 1, chunk)]
         for stage, share in enumerate(shares[1:], 2):
-            time += share * step + pause
+            time += share * step + pause + (2 if stage == 3 and chunk == len(steps) - 3 else 0)
             turns.append((time, stage, chunk))
     held = [[None] * len(steps) for _ in range(len(stages) + 1)]
     for _, stage, chunk in sorted(turns):

time: 226 us -> 231 us (1.022); the launches traced: 225 us -> 227 us
  starting transfers between devices: 88 us -> 96.5 us
  waiting for transfers between devices: 99.4 us -> 92.6 us
    ppermute x15, waiting for transfers between devices: 7.04 us -> 21.3 us  [second(): received.append(lax.ppermute(share, 'group', circle) if way > 0 else share)]
    ppermute x11, waiting for transfers between devices: 36.2 us -> 25.3 us  [hop_x(): return lax.ppermute(array, 'member', pairs)]
    ppermute x16, waiting for transfers between devices: 56.1 us -> 46 us  [hop(): return lax.ppermute(array, 'member', pairs)]
    ppermute x15, starting transfers between devices: 10.8 us -> 16.1 us  [second(): received.append(lax.ppermute(share, 'group', circle) if way > 0 else share)]
    ppermute x11, starting transfers between devices: 9.76 us -> 12.9 us  [hop_x(): return lax.ppermute(array, 'member', pairs)]
  transfers between devices with their start and end apart: 49 -> 49, of which waited for: 23 -> 25; matrix products, arithmetic and copies ran while one was open for 2% -> 2% of each run, Pallas kernels for 7% -> 7%
where the time goes in v1:
time: 231 us; the launch traced here: 227 us
  starting transfers between devices  96.5 us (42%)
  waiting for transfers between devices  92.6 us (40%)
  Pallas kernels  26.7 us (12%)
  local copies, waits for them, and re-layouts  4.93 us (2%)
  other arithmetic  4.73 us (2%)
    ppermute x16, starting transfers between devices, hop(): return lax.ppermute(array, 'member', pairs)  57.2 us
    ppermute x16, waiting for transfers between devices, hop(): return lax.ppermute(array, 'member', pairs)  46 us
    ppermute x11, waiting for transfers between devices, hop_x(): return lax.ppermute(array, 'member', pairs)  25.3 us
    ppermute x15, waiting for transfers between devices, second(): received.append(lax.ppermute(share, 'group', circle) if way > 0 else share)  21.3 us
    ppermute x15, starting transfers between devices, second(): received.append(lax.ppermute(share, 'group', circle) if way > 0 else share)  16.1 us
    pallas_call x20, Pallas kernels, whole(): pl.pallas_call(kernel, out_shape=out_shapes, in_specs=[pl.BlockSpec(memor...  14 us
    ppermute x11, starting transfers between devices, hop_x(): return lax.ppermute(array, 'member', pairs)  12.9 us
    pallas_call x1, Pallas kernels, prepare(): pl.pallas_call(functools.partial(prepare_kernel, x_count), out_shape=[jax...  7.11 us
  transfers between devices with their start and end apart: 49, of which 25 were waited for; matrix products, arithmetic and copies ran while one was open for 2% of the time, Pallas kernels for 7%

profile of v1, /device:TPU:0, one launch (start us, length us, event | category | flops | bytes accessed | tf_op | source)
XLA Modules:
  0.0 226.7 jit_solution(4204371744436831917)
XLA Ops:
  0.6 3.0 %collective-permute-start.1 = (f32[16,128]{1,0:T(8,128)}, f32[16,128]{1,0:T(8,128)S(1)}, u32[]{:S(2)}, u32[]{:S(2)}) collective-permute-start(f32[16,128]{1,0:T(8,128)} %param.21), channel_id=1, source_target_pairs={{0,1},{1,2},{2,3},{3,4},{4,5},{5,6},{6,7},{7,8},{8,9},{9,10},{10,1... | collective-permute-start | bytes 24584 | tf_op jit(solution)/shard_map/ppermute | solution.py:297
  3.6 3.5 %collective-permute-start.2 = (f32[16,128]{1,0:T(8,128)}, f32[16,128]{1,0:T(8,128)S(1)}, u32[]{:S(2)}, u32[]{:S(2)}) collective-permute-start(f32[16,128]{1,0:T(8,128)} %param.21), channel_id=1, source_target_pairs={{0,31},{1,0},{2,1},{3,2},{4,3},{5,4},{6,5},{7,6},{8,7},{9,8},{10,9... | collective-permute-start | bytes 24584 | tf_op jit(solution)/shard_map/ppermute | solution.py:298
  7.1 3.7 %collective-permute-done = s32[16]{0:T(128)S(1)} collective-permute-done((s32[16]{0:T(128)}, s32[16]{0:T(128)S(1)}, u32[]{:S(2)}, u32[]{:S(2)}) %collective-permute-start) | collective-permute-done | bytes 96 | tf_op jit(solution)/shard_map/ppermute | solution.py:358
  12.3 2.5 %copy-done = f32[16,5,128,128]{3,2,1,0:T(8,128)S(1)} copy-done((f32[16,5,128,128]{3,2,1,0:T(8,128)S(1)}, f32[16,5,128,128]{3,2,1,0:T(8,128)}, u32[]{:S(2)}) %copy-start) | copy-done | bytes 5242904
  15.6 7.1 %prepare.1 = (f32[16,5,8,128]{3,2,1,0:T(8,128)S(1)}, f32[16,5,16,128]{3,2,1,0:T(8,128)}, f32[16,5,16,128]{3,2,1,0:T(8,128)}, f32[16,5,16,128]{3,2,1,0:T(8,128)},...) custom-call(s32[16,5]{1,0:T(8,128)S(1)} %copy.16.slot_ref, ...), custom_call_target="tpu_custom_call" | custom-call | flops 2684354560 | bytes 10485760 | tf_op jit(solution)/shard_map/prepare/pallas_call | solution.py:96
  22.7 2.0 collective-permute-start.3
  24.7 6.2 %collective-permute-done.7.refs_1_ = f32[16,5,8,128]{3,2,1,0:T(8,128)S(1)} collective-permute-done((f32[16,5,8,128]{3,2,1,0:T(8,128)S(1)}, f32[16,5,8,128]{3,2,1,0:T(8,128)S(1)}, u32[]{:S(2)}, u32[]{:S(2)}) %collective-permute-start.7) | collective-permute-done | bytes 327712 | tf_op jit(solution)/shard_map/ppermute | solution.py:358
  34.2 3.2 %collective-permute-done.4 = s32[2,16]{1,0:T(2,128)S(1)} collective-permute-done((s32[2,16]{1,0:T(2,128)S(1)}, s32[2,16]{1,0:T(2,128)S(1)}, u32[]{:S(2)}, u32[]{:S(2)}) %collective-permute-start.4) | collective-permute-done | bytes 160 | tf_op jit(solution)/shard_map/ppermute | solution.py:350
  37.4 5.4 %collective-permute-start.5 = (f32[16,5,16,128]{3,2,1,0:T(8,128)}, f32[16,5,16,128]{3,2,1,0:T(8,128)}, u32[]{:S(2)}, u32[]{:S(2)}) collective-permute-start(f32[16,5,16,128]{3,2,1,0:T(8,128)} %get-tuple-element.209.refs_0_), channel_id=1, source_target_pairs={{0,2},{1,3},{6,4},{7,5},{8,10},{9,11},{14,12},{15,13},{16,18},{17,... | collective-permute-start | bytes 1966088 | tf_op jit(solution)/shard_map/ppermute | solution.py:350
  42.8 1.9 combine.5
  45.6 1.4 collective-permute-start.18
  47.1 3.3 %collective-permute-done.11.refs_1_ = f32[16,5,16,128]{3,2,1,0:T(8,128)} collective-permute-done((f32[16,5,16,128]{3,2,1,0:T(8,128)}, f32[16,5,16,128]{3,2,1,0:T(8,128)}, u32[]{:S(2)}, u32[]{:S(2)}) %collective-permute-start.11) | collective-permute-done | bytes 655392 | tf_op jit(solution)/shard_map/ppermute | solution.py:358
  50.4 3.4 %collective-permute-start.12 = (f32[16,5,16,128]{3,2,1,0:T(8,128)}, f32[16,5,16,128]{3,2,1,0:T(8,128)}, u32[]{:S(2)}, u32[]{:S(2)}) collective-permute-start(f32[16,5,16,128]{3,2,1,0:T(8,128)} %collective-permute-done.11.refs_1_), channel_id=1, source_target_pairs={{0,2},{1,3},{6,4},{7,5},{8,10},{9,11},{14,12},{15,13},{16,18},{17,... | collective-permute-start | bytes 1966088 | tf_op jit(solution)/shard_map/ppermute | solution.py:350
  54.3 5.2 %collective-permute-start.6 = (f32[16,5,16,128]{3,2,1,0:T(8,128)S(1)}, f32[16,5,16,128]{3,2,1,0:T(8,128)}, u32[]{:S(2)}, u32[]{:S(2)}) collective-permute-start(f32[16,5,16,128]{3,2,1,0:T(8,128)S(1)} %copy-done.4), channel_id=1, source_target_pairs={{0,2},{1,3},{6,4},{7,5},{8,10},{9,11},{14,12},{15,13},{16,18},{17,... | collective-permute-start | bytes 1966088 | tf_op jit(solution)/shard_map/ppermute | solution.py:350
  60.5 3.0 %multiply_reduce_fusion = f32[16,128]{1,0:T(8,128)S(1)} fusion(f32[16,5,128,128]{3,2,1,0:T(8,128)} %fine_ref.1, f32[16,5,128]{2,1,0:T(8,128)S(1)} %reshape.12), kind=kLoop, calls=%fused_computation.1 | loop fusion | flops 2619392 | bytes 5292032 | tf_op jit(solution)/shard_map/reduce_sum | solution.py:310
  64.5 3.9 %collective-permute-done.12.refs_3_ = f32[16,5,16,128]{3,2,1,0:T(8,128)} collective-permute-done((f32[16,5,16,128]{3,2,1,0:T(8,128)}, f32[16,5,16,128]{3,2,1,0:T(8,128)}, u32[]{:S(2)}, u32[]{:S(2)}) %collective-permute-start.12) | collective-permute-done | bytes 655392 | tf_op jit(solution)/shard_map/ppermute | solution.py:350
  68.4 2.4 %combine.6 = (f32[32,5,16,128]{3,2,1,0:T(8,128)S(1)}, f32[64,5,16,128]{3,2,1,0:T(8,128)S(1)}) custom-call(s32[4,16]{1,0:T(4,128)S(1)} %fusion.7.target_ref, f32[16,5,16,128]{3,2,1,0:T(8,128)} %get-tuple-element.209.refs_0_, f32[16,5,16,128]{3,2,1,0:T(8,128)} %collective-permute-done.11.refs_1_, f32[16,5,16,128]{3,2,1,0:T(8,128)} %collective-permute-done.5.refs_2_, ...), custom_call_target="tpu_custom_call" | custom-call | flops 6000000000 | tf_op jit(solution)/shard_map/combine/pallas_call | solution.py:135
  71.6 13.3 %collective-permute-start.19 = (f32[16,5,16,128]{3,2,1,0:T(8,128)}, f32[16,5,16,128]{3,2,1,0:T(8,128)S(1)}, u32[]{:S(2)}, u32[]{:S(2)}) collective-permute-start(f32[16,5,16,128]{3,2,1,0:T(8,128)} %collective-permute-done.18.refs_1_), channel_id=1, source_target_pairs={{0,2},{1,3},{6,4},{7,5},{8,10},{9,11},{14,12},{15,13},{16,18},{17,... | collective-permute-start | bytes 1966088 | tf_op jit(solution)/shard_map/ppermute | solution.py:350
  87.1 6.7 %collective-permute-done.10.refs_2_ = f32[16,5,8,128]{3,2,1,0:T(8,128)S(1)} collective-permute-done((f32[16,5,8,128]{3,2,1,0:T(8,128)S(1)}, f32[16,5,8,128]{3,2,1,0:T(8,128)S(1)}, u32[]{:S(2)}, u32[]{:S(2)}) %collective-permute-start.10) | collective-permute-done | bytes 327712 | tf_op jit(solution)/shard_map/ppermute | solution.py:350
  93.9 1.3 collective-permute-start.13
  95.2 1.5 collective-permute-start.23
  96.7 6.6 %collective-permute-done.13.refs_1_.refs_5_ = f32[8,5,8,128]{3,2,1,0:T(8,128)S(1)} collective-permute-done((f32[8,5,8,128]{3,2,1,0:T(8,128)S(1)}, f32[8,5,8,128]{3,2,1,0:T(8,128)S(1)}, u32[]{:S(2)}, u32[]{:S(2)}) %collective-permute-start.13) | collective-permute-done | bytes 163872 | tf_op jit(solution)/shard_map/ppermute | solution.py:358
  104.2 2.0 combine.7
  107.7 4.6 %collective-permute-start.24 = (f32[16,5,16,128]{3,2,1,0:T(8,128)S(1)}, f32[16,5,16,128]{3,2,1,0:T(8,128)S(1)}, u32[]{:S(2)}, u32[]{:S(2)}) collective-permute-start(f32[16,5,16,128]{3,2,1,0:T(8,128)S(1)} %collective-permute-done.22.refs_1_), channel_id=1, source_target_pairs={{0,2},{1,3},{6,4},{7,5},{8,10},{9,11},{14,12},{15,13},{16,18},{17,... | collective-permute-start | bytes 1966088 | tf_op jit(solution)/shard_map/ppermute | solution.py:350
  113.1 2.2 collective-permute-start.30
  115.3 5.7 %collective-permute-done.20.refs_2_ = f32[16,5,16,128]{3,2,1,0:T(8,128)S(1)} collective-permute-done((f32[16,5,16,128]{3,2,1,0:T(8,128)S(1)}, f32[16,5,16,128]{3,2,1,0:T(8,128)S(1)}, u32[]{:S(2)}, u32[]{:S(2)}) %collective-permute-start.20) | collective-permute-done | bytes 655392 | tf_op jit(solution)/shard_map/ppermute | solution.py:350
  121.1 2.6 %collective-permute-done.24.refs_3_ = f32[16,5,16,128]{3,2,1,0:T(8,128)S(1)} collective-permute-done((f32[16,5,16,128]{3,2,1,0:T(8,128)S(1)}, f32[16,5,16,128]{3,2,1,0:T(8,128)S(1)}, u32[]{:S(2)}, u32[]{:S(2)}) %collective-permute-start.24) | collective-permute-done | bytes 655392 | tf_op jit(solution)/shard_map/ppermute | solution.py:350
  125.8 1.6 collective-permute-start.15
  127.4 1.4 collective-permute-start.16
  128.8 2.9 %collective-permute-done.14.refs_1_ = f32[4,5,16,128]{3,2,1,0:T(8,128)S(1)} collective-permute-done((f32[4,5,16,128]{3,2,1,0:T(8,128)S(1)}, f32[4,5,16,128]{3,2,1,0:T(8,128)S(1)}, u32[]{:S(2)}, u32[]{:S(2)}) %collective-permute-start.14) | collective-permute-done | bytes 163872 | tf_op jit(solution)/shard_map/ppermute | solution.py:466
  131.7 2.6 %collective-permute-start.21 = (f32[8,5,16,128]{3,2,1,0:T(8,128)S(1)}, f32[8,5,16,128]{3,2,1,0:T(8,128)S(1)}, u32[]{:S(2)}, u32[]{:S(2)}) collective-permute-start(f32[8,5,16,128]{3,2,1,0:T(8,128)S(1)} %get-tuple-element.244), channel_id=1, source_target_pairs={{0,1},{1,0},{2,3},{3,2},{4,5},{5,4},{6,7},{7,6},{8,9},{9,8},{10,11... | collective-permute-start | bytes 983048 | tf_op jit(solution)/shard_map/ppermute | solution.py:358
  134.3 11.5 %collective-permute-start.32 = (f32[16,5,8,128]{3,2,1,0:T(8,128)S(1)}, f32[16,5,8,128]{3,2,1,0:T(8,128)S(1)}, u32[]{:S(2)}, u32[]{:S(2)}) collective-permute-start(f32[16,5,8,128]{3,2,1,0:T(8,128)S(1)} %collective-permute-done.30.refs_1_), channel_id=1, source_target_pairs={{0,2},{1,3},{6,4},{7,5},{8,10},{9,11},{14,12},{15,13},{16,18},{17,... | collective-permute-start | bytes 983048 | tf_op jit(solution)/shard_map/ppermute | solution.py:350
  149.5 1.6 collective-permute-start.25
  151.1 1.9 collective-permute-done.32.refs_3_
  153.0 7.0 %collective-permute-done.31.refs_2_ = f32[16,5,8,128]{3,2,1,0:T(8,128)S(1)} collective-permute-done((f32[16,5,8,128]{3,2,1,0:T(8,128)S(1)}, f32[16,5,8,128]{3,2,1,0:T(8,128)S(1)}, u32[]{:S(2)}, u32[]{:S(2)}) %collective-permute-start.31) | collective-permute-done | bytes 327712 | tf_op jit(solution)/shard_map/ppermute | solution.py:350
  161.8 5.4 %collective-permute-done.29.refs_2_ = f32[16,5,16,128]{3,2,1,0:T(8,128)S(1)} collective-permute-done((f32[16,5,16,128]{3,2,1,0:T(8,128)S(1)}, f32[16,5,16,128]{3,2,1,0:T(8,128)S(1)}, u32[]{:S(2)}, u32[]{:S(2)}) %collective-permute-start.29) | collective-permute-done | bytes 655392 | tf_op jit(solution)/shard_map/ppermute | solution.py:350
  171.7 7.1 %collective-permute-done.26.refs_6_ = f32[4,5,32,128]{3,2,1,0:T(8,128)S(1)} collective-permute-done((f32[4,5,32,128]{3,2,1,0:T(8,128)S(1)}, f32[4,5,32,128]{3,2,1,0:T(8,128)S(1)}, u32[]{:S(2)}, u32[]{:S(2)}) %collective-permute-start.26) | collective-permute-done | bytes 327712 | tf_op jit(solution)/shard_map/ppermute | solution.py:466
  178.8 1.3 collective-permute-done.27.refs_7_
  181.0 2.4 %collective-permute-start.35 = (f32[4,5,32,128]{3,2,1,0:T(8,128)S(1)}, f32[4,5,32,128]{3,2,1,0:T(8,128)S(1)}, u32[]{:S(2)}, u32[]{:S(2)}) collective-permute-start(f32[4,5,32,128]{3,2,1,0:T(8,128)S(1)} %get-tuple-element.289), channel_id=1, source_target_pairs={{0,8},{8,16},{16,24},{24,0},{1,9},{9,17},{17,25},{25,1},{2,10},{10... | collective-permute-start | bytes 983048 | tf_op jit(solution)/shard_map/ppermute | solution.py:466
  187.7 9.0 %collective-permute-done.41.refs_2_ = f32[16,5,8,128]{3,2,1,0:T(8,128)S(1)} collective-permute-done((f32[16,5,8,128]{3,2,1,0:T(8,128)S(1)}, f32[16,5,8,128]{3,2,1,0:T(8,128)S(1)}, u32[]{:S(2)}, u32[]{:S(2)}) %collective-permute-start.41) | collective-permute-done | bytes 327712 | tf_op jit(solution)/shard_map/ppermute | solution.py:350
  199.4 1.7 collective-permute-start.43
  202.3 5.4 %collective-permute-done.45.refs_9_.refs_1_ = f32[8,5,8,128]{3,2,1,0:T(8,128)S(1)} collective-permute-done((f32[8,5,8,128]{3,2,1,0:T(8,128)S(1)}, f32[8,5,8,128]{3,2,1,0:T(8,128)S(1)}, u32[]{:S(2)}, u32[]{:S(2)}) %collective-permute-start.45) | collective-permute-done | bytes 163872 | tf_op jit(solution)/shard_map/ppermute | solution.py:358
  208.1 1.9 collective-permute-done.43.refs_14_
  210.0 3.9 %collective-permute-done.44.refs_15_ = f32[4,5,32,128]{3,2,1,0:T(8,128)S(1)} collective-permute-done((f32[4,5,32,128]{3,2,1,0:T(8,128)S(1)}, f32[4,5,32,128]{3,2,1,0:T(8,128)S(1)}, u32[]{:S(2)}, u32[]{:S(2)}) %collective-permute-start.44) | collective-permute-done | bytes 327712 | tf_op jit(solution)/shard_map/ppermute | solution.py:466
  214.7 2.1 collective-permute-start.46
  218.2 3.1 %place_one.1 = f32[8,5,128,128]{3,2,1,0:T(8,128)} custom-call(s32[1]{0:T(128)} %bitcast.place_ref, f32[8,5,8,128]{3,2,1,0:T(8,128)S(1)} %get-tuple-element.221.refs_0_, f32[8,5,16,128]{3,2,1,0:T(8,128)S(1)} %get-tuple-element.256.refs_0_.refs_1_, f32[8,5,16,128]{3,2,1,0:T(8,128)S(1)} %get-tuple-element.286.refs_0_.refs_2_, ...), custom_call_target="tpu_custom_call" | custom-call | bytes 5242880 | tf_op jit(solution)/shard_map/place_one/pallas_call | solution.py:219
  221.3 1.9 collective-permute-done.47.refs_18_
  224.2 2.6 %last.1 = f32[4,5,128,128]{3,2,1,0:T(8,128)} custom-call(s32[1]{0:T(128)} %bitcast.place_ref, f32[128,128]{1,0:T(8,128)S(1)} %copy-done.2, f32[4,5,16,128]{3,2,1,0:T(8,128)S(1)} %get-tuple-element.320.refs_0_, f32[4,5,16,128]{3,2,1,0:T(8,128)S(1)} %collective-permute-done.14.refs_1_, f32[4,5,16,128]{3,2,1,0:T(8,128)S(1)} %collective-permute-done.15.refs_2_, ...), custom_call_target="tpu_custom_call" | custom-call | flops 671088640 | bytes 6553600 | tf_op jit(solution)/shard_map/last/pallas_call | solution.py:266
  (116 shorter events, 39.7 us)
Async XLA Ops:
  0.6 10.8 %collective-permute-start.1 = (f32[16,128]{1,0:T(8,128)}, f32[16,128]{1,0:T(8,128)S(1)}, u32[]{:S(2)}, u32[]{:S(2)}) collective-permute-start(f32[16,128]{1,0:T(8,128)} %param.21), channel_id=1, source_target_pairs={{0,1},{1,2},{2,3},{3,4},{4,5},{5,6},{6,7},{7,8},{8,9},{9,10},{10,1... | collective-permute-start | bytes 24584 | tf_op jit(solution)/shard_map/ppermute | solution.py:297
  3.6 7.8 %collective-permute-start.2 = (f32[16,128]{1,0:T(8,128)}, f32[16,128]{1,0:T(8,128)S(1)}, u32[]{:S(2)}, u32[]{:S(2)}) collective-permute-start(f32[16,128]{1,0:T(8,128)} %param.21), channel_id=1, source_target_pairs={{0,31},{1,0},{2,1},{3,2},{4,3},{5,4},{6,5},{7,6},{8,7},{9,8},{10,9... | collective-permute-start | bytes 24584 | tf_op jit(solution)/shard_map/ppermute | solution.py:298
  22.7 8.2 %collective-permute-start.7 = (f32[16,5,8,128]{3,2,1,0:T(8,128)S(1)}, f32[16,5,8,128]{3,2,1,0:T(8,128)S(1)}, u32[]{:S(2)}, u32[]{:S(2)}) collective-permute-start(f32[16,5,8,128]{3,2,1,0:T(8,128)S(1)} %get-tuple-element.182), channel_id=1, source_target_pairs={{0,1},{1,0},{2,3},{3,2},{4,5},{5,4},{6,7},{7,6},{8,9},{9,8},{10,11... | collective-permute-start | bytes 983048 | tf_op jit(solution)/shard_map/ppermute | solution.py:358
  22.7 14.7 %collective-permute-start.3 = (f32[16,5,8,128]{3,2,1,0:T(8,128)S(1)}, f32[16,5,8,128]{3,2,1,0:T(8,128)S(1)}, u32[]{:S(2)}, u32[]{:S(2)}) collective-permute-start(f32[16,5,8,128]{3,2,1,0:T(8,128)S(1)} %get-tuple-element.184.refs_0_), channel_id=1, source_target_pairs={{0,2},{1,3},{6,4},{7,5},{8,10},{9,11},{14,12},{15,13},{16,18},{17,... | collective-permute-start | bytes 983048 | tf_op jit(solution)/shard_map/ppermute | solution.py:350
  30.9 12.0 %collective-permute-start.8 = (f32[16,5,8,128]{3,2,1,0:T(8,128)S(1)}, f32[16,5,8,128]{3,2,1,0:T(8,128)S(1)}, u32[]{:S(2)}, u32[]{:S(2)}) collective-permute-start(f32[16,5,8,128]{3,2,1,0:T(8,128)S(1)} %collective-permute-done.7.refs_1_), channel_id=1, source_target_pairs={{0,2},{1,3},{6,4},{7,5},{8,10},{9,11},{14,12},{15,13},{16,18},{17,... | collective-permute-start | bytes 983048 | tf_op jit(solution)/shard_map/ppermute | solution.py:350
  32.2 5.2 %collective-permute-start.4 = (s32[2,16]{1,0:T(2,128)S(1)}, s32[2,16]{1,0:T(2,128)S(1)}, u32[]{:S(2)}, u32[]{:S(2)}) collective-permute-start(s32[2,16]{1,0:T(2,128)S(1)} %pad_add_fusion.1), channel_id=1, source_target_pairs={{0,2},{1,3},{6,4},{7,5},{8,10},{9,11},{14,12},{15,13},{16,18},{17,... | collective-permute-start | bytes 392 | tf_op jit(solution)/shard_map/ppermute | solution.py:350
  33.5 16.9 %collective-permute-start.11 = (f32[16,5,16,128]{3,2,1,0:T(8,128)}, f32[16,5,16,128]{3,2,1,0:T(8,128)}, u32[]{:S(2)}, u32[]{:S(2)}) collective-permute-start(f32[16,5,16,128]{3,2,1,0:T(8,128)} %get-tuple-element.199), channel_id=1, source_target_pairs={{0,1},{1,0},{2,3},{3,2},{4,5},{5,4},{6,7},{7,6},{8,9},{9,8},{10,11... | collective-permute-start | bytes 1966088 | tf_op jit(solution)/shard_map/ppermute | solution.py:358
  37.4 16.9 %collective-permute-start.5 = (f32[16,5,16,128]{3,2,1,0:T(8,128)}, f32[16,5,16,128]{3,2,1,0:T(8,128)}, u32[]{:S(2)}, u32[]{:S(2)}) collective-permute-start(f32[16,5,16,128]{3,2,1,0:T(8,128)} %get-tuple-element.209.refs_0_), channel_id=1, source_target_pairs={{0,2},{1,3},{6,4},{7,5},{8,10},{9,11},{14,12},{15,13},{16,18},{17,... | collective-permute-start | bytes 1966088 | tf_op jit(solution)/shard_map/ppermute | solution.py:350
  44.7 14.8 %collective-permute-start.9 = (f32[32,5,8,128]{3,2,1,0:T(8,128)}, f32[32,5,8,128]{3,2,1,0:T(8,128)S(1)}, u32[]{:S(2)}, u32[]{:S(2)}) collective-permute-start(f32[32,5,8,128]{3,2,1,0:T(8,128)} %get-tuple-element.189), channel_id=1, source_target_pairs={{2,4},{3,5},{4,2},{5,3},{10,12},{11,13},{12,10},{13,11},{18,20},{1... | collective-permute-start | bytes 1966088 | tf_op jit(solution)/shard_map/ppermute | solution.py:426
  45.6 26.0 %collective-permute-start.18 = (f32[16,5,16,128]{3,2,1,0:T(8,128)}, f32[16,5,16,128]{3,2,1,0:T(8,128)}, u32[]{:S(2)}, u32[]{:S(2)}) collective-permute-start(f32[16,5,16,128]{3,2,1,0:T(8,128)} %get-tuple-element.228), channel_id=1, source_target_pairs={{0,1},{1,0},{2,3},{3,2},{4,5},{5,4},{6,7},{7,6},{8,9},{9,8},{10,11... | collective-permute-start | bytes 1966088 | tf_op jit(solution)/shard_map/ppermute | solution.py:358
  50.4 18.0 %collective-permute-start.12 = (f32[16,5,16,128]{3,2,1,0:T(8,128)}, f32[16,5,16,128]{3,2,1,0:T(8,128)}, u32[]{:S(2)}, u32[]{:S(2)}) collective-permute-start(f32[16,5,16,128]{3,2,1,0:T(8,128)} %collective-permute-done.11.refs_1_), channel_id=1, source_target_pairs={{0,2},{1,3},{6,4},{7,5},{8,10},{9,11},{14,12},{15,13},{16,18},{17,... | collective-permute-start | bytes 1966088 | tf_op jit(solution)/shard_map/ppermute | solution.py:350
  54.3 32.8 %collective-permute-start.6 = (f32[16,5,16,128]{3,2,1,0:T(8,128)S(1)}, f32[16,5,16,128]{3,2,1,0:T(8,128)}, u32[]{:S(2)}, u32[]{:S(2)}) collective-permute-start(f32[16,5,16,128]{3,2,1,0:T(8,128)S(1)} %copy-done.4), channel_id=1, source_target_pairs={{0,2},{1,3},{6,4},{7,5},{8,10},{9,11},{14,12},{15,13},{16,18},{17,... | collective-permute-start | bytes 1966088 | tf_op jit(solution)/shard_map/ppermute | solution.py:350
  70.8 35.4 %collective-permute-start.17 = (f32[32,5,16,128]{3,2,1,0:T(8,128)S(1)}, f32[32,5,16,128]{3,2,1,0:T(8,128)S(1)}, u32[]{:S(2)}, u32[]{:S(2)}) collective-permute-start(f32[32,5,16,128]{3,2,1,0:T(8,128)S(1)} %get-tuple-element.213), channel_id=1, source_target_pairs={{2,4},{3,5},{4,2},{5,3},{10,12},{11,13},{12,10},{13,11},{18,20},{1... | collective-permute-start | bytes 3932168 | tf_op jit(solution)/shard_map/ppermute | solution.py:426
  71.6 32.6 %collective-permute-start.19 = (f32[16,5,16,128]{3,2,1,0:T(8,128)}, f32[16,5,16,128]{3,2,1,0:T(8,128)S(1)}, u32[]{:S(2)}, u32[]{:S(2)}) collective-permute-start(f32[16,5,16,128]{3,2,1,0:T(8,128)} %collective-permute-done.18.refs_1_), channel_id=1, source_target_pairs={{0,2},{1,3},{6,4},{7,5},{8,10},{9,11},{14,12},{15,13},{16,18},{17,... | collective-permute-start | bytes 1966088 | tf_op jit(solution)/shard_map/ppermute | solution.py:350
  84.8 9.0 %collective-permute-start.10 = (f32[16,5,8,128]{3,2,1,0:T(8,128)S(1)}, f32[16,5,8,128]{3,2,1,0:T(8,128)S(1)}, u32[]{:S(2)}, u32[]{:S(2)}) collective-permute-start(f32[16,5,8,128]{3,2,1,0:T(8,128)S(1)} %get-tuple-element.194), channel_id=1, source_target_pairs={{2,0},{3,1},{4,6},{5,7},{10,8},{11,9},{12,14},{13,15},{18,16},{19,... | collective-permute-start | bytes 983048 | tf_op jit(solution)/shard_map/ppermute | solution.py:350
  86.2 21.6 %collective-permute-start.22 = (f32[16,5,16,128]{3,2,1,0:T(8,128)S(1)}, f32[16,5,16,128]{3,2,1,0:T(8,128)S(1)}, u32[]{:S(2)}, u32[]{:S(2)}) collective-permute-start(f32[16,5,16,128]{3,2,1,0:T(8,128)S(1)} %copy-done.11), channel_id=1, source_target_pairs={{0,1},{1,0},{2,3},{3,2},{4,5},{5,4},{6,7},{7,6},{8,9},{9,8},{10,11... | collective-permute-start | bytes 1966088 | tf_op jit(solution)/shard_map/ppermute | solution.py:358
  93.9 9.5 %collective-permute-start.13 = (f32[8,5,8,128]{3,2,1,0:T(8,128)S(1)}, f32[8,5,8,128]{3,2,1,0:T(8,128)S(1)}, u32[]{:S(2)}, u32[]{:S(2)}) collective-permute-start(f32[8,5,8,128]{3,2,1,0:T(8,128)S(1)} %get-tuple-element.218), channel_id=1, source_target_pairs={{0,1},{1,0},{2,3},{3,2},{4,5},{5,4},{6,7},{7,6},{8,9},{9,8},{10,11... | collective-permute-start | bytes 491528 | tf_op jit(solution)/shard_map/ppermute | solution.py:358
  95.2 20.1 %collective-permute-start.23 = (f32[16,5,16,128]{3,2,1,0:T(8,128)S(1)}, f32[16,5,16,128]{3,2,1,0:T(8,128)S(1)}, u32[]{:S(2)}, u32[]{:S(2)}) collective-permute-start(f32[16,5,16,128]{3,2,1,0:T(8,128)S(1)} %copy-done.3), channel_id=1, source_target_pairs={{0,2},{1,3},{6,4},{7,5},{8,10},{9,11},{14,12},{15,13},{16,18},{17,... | collective-permute-start | bytes 1966088 | tf_op jit(solution)/shard_map/ppermute | solution.py:350
  106.4 14.7 %collective-permute-start.20 = (f32[16,5,16,128]{3,2,1,0:T(8,128)S(1)}, f32[16,5,16,128]{3,2,1,0:T(8,128)S(1)}, u32[]{:S(2)}, u32[]{:S(2)}) collective-permute-start(f32[16,5,16,128]{3,2,1,0:T(8,128)S(1)} %get-tuple-element.239), channel_id=1, source_target_pairs={{2,0},{3,1},{4,6},{5,7},{10,8},{11,9},{12,14},{13,15},{18,16},{19,... | collective-permute-start | bytes 1966088 | tf_op jit(solution)/shard_map/ppermute | solution.py:350
  107.7 16.0 %collective-permute-start.24 = (f32[16,5,16,128]{3,2,1,0:T(8,128)S(1)}, f32[16,5,16,128]{3,2,1,0:T(8,128)S(1)}, u32[]{:S(2)}, u32[]{:S(2)}) collective-permute-start(f32[16,5,16,128]{3,2,1,0:T(8,128)S(1)} %collective-permute-done.22.refs_1_), channel_id=1, source_target_pairs={{0,2},{1,3},{6,4},{7,5},{8,10},{9,11},{14,12},{15,13},{16,18},{17,... | collective-permute-start | bytes 1966088 | tf_op jit(solution)/shard_map/ppermute | solution.py:350
  112.3 35.7 %collective-permute-start.28 = (f32[32,5,16,128]{3,2,1,0:T(8,128)S(1)}, f32[32,5,16,128]{3,2,1,0:T(8,128)S(1)}, u32[]{:S(2)}, u32[]{:S(2)}) collective-permute-start(f32[32,5,16,128]{3,2,1,0:T(8,128)S(1)} %get-tuple-element.234), channel_id=1, source_target_pairs={{2,4},{3,5},{4,2},{5,3},{10,12},{11,13},{12,10},{13,11},{18,20},{1... | collective-permute-start | bytes 3932168 | tf_op jit(solution)/shard_map/ppermute | solution.py:426
  113.1 14.3 %collective-permute-start.30 = (f32[16,5,8,128]{3,2,1,0:T(8,128)S(1)}, f32[16,5,8,128]{3,2,1,0:T(8,128)S(1)}, u32[]{:S(2)}, u32[]{:S(2)}) collective-permute-start(f32[16,5,8,128]{3,2,1,0:T(8,128)S(1)} %copy-done.12), channel_id=1, source_target_pairs={{0,1},{1,0},{2,3},{3,2},{4,5},{5,4},{6,7},{7,6},{8,9},{9,8},{10,11... | collective-permute-start | bytes 983048 | tf_op jit(solution)/shard_map/ppermute | solution.py:358
  125.0 42.3 %collective-permute-start.34 = (f32[32,5,16,128]{3,2,1,0:T(8,128)S(1)}, f32[32,5,16,128]{3,2,1,0:T(8,128)S(1)}, u32[]{:S(2)}, u32[]{:S(2)}) collective-permute-start(f32[32,5,16,128]{3,2,1,0:T(8,128)S(1)} %get-tuple-element.255), channel_id=1, source_target_pairs={{2,4},{3,5},{4,2},{5,3},{10,12},{11,13},{12,10},{13,11},{18,20},{1... | collective-permute-start | bytes 3932168 | tf_op jit(solution)/shard_map/ppermute | solution.py:426
  125.8 5.9 %collective-permute-start.14 = (f32[4,5,16,128]{3,2,1,0:T(8,128)S(1)}, f32[4,5,16,128]{3,2,1,0:T(8,128)S(1)}, u32[]{:S(2)}, u32[]{:S(2)}) collective-permute-start(f32[4,5,16,128]{3,2,1,0:T(8,128)S(1)} %get-tuple-element.224), channel_id=1, source_target_pairs={{0,8},{8,16},{16,24},{24,0},{1,9},{9,17},{17,25},{25,1},{2,10},{10... | collective-permute-start | bytes 491528 | tf_op jit(solution)/shard_map/ppermute | solution.py:466
  125.8 8.5 %collective-permute-start.15 = (f32[4,5,16,128]{3,2,1,0:T(8,128)S(1)}, f32[4,5,16,128]{3,2,1,0:T(8,128)S(1)}, u32[]{:S(2)}, u32[]{:S(2)}) collective-permute-start(f32[4,5,16,128]{3,2,1,0:T(8,128)S(1)} %get-tuple-element.225), channel_id=1, source_target_pairs={{0,16},{8,24},{16,0},{24,8},{1,17},{9,25},{17,1},{25,9},{2,18},{10... | collective-permute-start | bytes 491528 | tf_op jit(solution)/shard_map/ppermute | solution.py:466
  127.4 18.3 %collective-permute-start.16 = (f32[4,5,16,128]{3,2,1,0:T(8,128)S(1)}, f32[4,5,16,128]{3,2,1,0:T(8,128)S(1)}, u32[]{:S(2)}, u32[]{:S(2)}) collective-permute-start(f32[4,5,16,128]{3,2,1,0:T(8,128)S(1)} %get-tuple-element.226), channel_id=1, source_target_pairs={{0,24},{8,0},{16,8},{24,16},{1,25},{9,1},{17,9},{25,17},{2,26},{10... | collective-permute-start | bytes 491528 | tf_op jit(solution)/shard_map/ppermute | solution.py:466
  131.7 15.4 %collective-permute-start.21 = (f32[8,5,16,128]{3,2,1,0:T(8,128)S(1)}, f32[8,5,16,128]{3,2,1,0:T(8,128)S(1)}, u32[]{:S(2)}, u32[]{:S(2)}) collective-permute-start(f32[8,5,16,128]{3,2,1,0:T(8,128)S(1)} %get-tuple-element.244), channel_id=1, source_target_pairs={{0,1},{1,0},{2,3},{3,2},{4,5},{5,4},{6,7},{7,6},{8,9},{9,8},{10,11... | collective-permute-start | bytes 983048 | tf_op jit(solution)/shard_map/ppermute | solution.py:358
  134.3 18.7 %collective-permute-start.32 = (f32[16,5,8,128]{3,2,1,0:T(8,128)S(1)}, f32[16,5,8,128]{3,2,1,0:T(8,128)S(1)}, u32[]{:S(2)}, u32[]{:S(2)}) collective-permute-start(f32[16,5,8,128]{3,2,1,0:T(8,128)S(1)} %collective-permute-done.30.refs_1_), channel_id=1, source_target_pairs={{0,2},{1,3},{6,4},{7,5},{8,10},{9,11},{14,12},{15,13},{16,18},{17,... | collective-permute-start | bytes 983048 | tf_op jit(solution)/shard_map/ppermute | solution.py:350
  145.8 14.2 %collective-permute-start.31 = (f32[16,5,8,128]{3,2,1,0:T(8,128)S(1)}, f32[16,5,8,128]{3,2,1,0:T(8,128)S(1)}, u32[]{:S(2)}, u32[]{:S(2)}) collective-permute-start(f32[16,5,8,128]{3,2,1,0:T(8,128)S(1)} %copy-done.5), channel_id=1, source_target_pairs={{0,2},{1,3},{6,4},{7,5},{8,10},{9,11},{14,12},{15,13},{16,18},{17,... | collective-permute-start | bytes 983048 | tf_op jit(solution)/shard_map/ppermute | solution.py:350
  148.2 19.0 %collective-permute-start.29 = (f32[16,5,16,128]{3,2,1,0:T(8,128)S(1)}, f32[16,5,16,128]{3,2,1,0:T(8,128)S(1)}, u32[]{:S(2)}, u32[]{:S(2)}) collective-permute-start(f32[16,5,16,128]{3,2,1,0:T(8,128)S(1)} %get-tuple-element.267), channel_id=1, source_target_pairs={{2,0},{3,1},{4,6},{5,7},{10,8},{11,9},{12,14},{13,15},{18,16},{19,... | collective-permute-start | bytes 1966088 | tf_op jit(solution)/shard_map/ppermute | solution.py:350
  149.5 21.0 %collective-permute-start.25 = (f32[4,5,32,128]{3,2,1,0:T(8,128)S(1)}, f32[4,5,32,128]{3,2,1,0:T(8,128)S(1)}, u32[]{:S(2)}, u32[]{:S(2)}) collective-permute-start(f32[4,5,32,128]{3,2,1,0:T(8,128)S(1)} %get-tuple-element.259), channel_id=1, source_target_pairs={{0,8},{8,16},{16,24},{24,0},{1,9},{9,17},{17,25},{25,1},{2,10},{10... | collective-permute-start | bytes 983048 | tf_op jit(solution)/shard_map/ppermute | solution.py:466
  161.1 22.6 %collective-permute-start.39 = (f32[32,5,8,128]{3,2,1,0:T(8,128)S(1)}, f32[32,5,8,128]{3,2,1,0:T(8,128)S(1)}, u32[]{:S(2)}, u32[]{:S(2)}) collective-permute-start(f32[32,5,8,128]{3,2,1,0:T(8,128)S(1)} %get-tuple-element.274), channel_id=1, source_target_pairs={{2,4},{3,5},{4,2},{5,3},{10,12},{11,13},{12,10},{13,11},{18,20},{1... | collective-permute-start | bytes 1966088 | tf_op jit(solution)/shard_map/ppermute | solution.py:426
  167.4 18.9 %collective-permute-start.38 = (f32[16,5,16,128]{3,2,1,0:T(8,128)S(1)}, f32[16,5,16,128]{3,2,1,0:T(8,128)S(1)}, u32[]{:S(2)}, u32[]{:S(2)}) collective-permute-start(f32[16,5,16,128]{3,2,1,0:T(8,128)S(1)} %get-tuple-element.285), channel_id=1, source_target_pairs={{2,0},{3,1},{4,6},{5,7},{10,8},{11,9},{12,14},{13,15},{18,16},{19,... | collective-permute-start | bytes 1966088 | tf_op jit(solution)/shard_map/ppermute | solution.py:350
  168.7 10.0 %collective-permute-start.26 = (f32[4,5,32,128]{3,2,1,0:T(8,128)S(1)}, f32[4,5,32,128]{3,2,1,0:T(8,128)S(1)}, u32[]{:S(2)}, u32[]{:S(2)}) collective-permute-start(f32[4,5,32,128]{3,2,1,0:T(8,128)S(1)} %get-tuple-element.260), channel_id=1, source_target_pairs={{0,16},{8,24},{16,0},{24,8},{1,17},{9,25},{17,1},{25,9},{2,18},{10... | collective-permute-start | bytes 983048 | tf_op jit(solution)/shard_map/ppermute | solution.py:466
  169.7 10.4 %collective-permute-start.27 = (f32[4,5,32,128]{3,2,1,0:T(8,128)S(1)}, f32[4,5,32,128]{3,2,1,0:T(8,128)S(1)}, u32[]{:S(2)}, u32[]{:S(2)}) collective-permute-start(f32[4,5,32,128]{3,2,1,0:T(8,128)S(1)} %get-tuple-element.261), channel_id=1, source_target_pairs={{0,24},{8,0},{16,8},{24,16},{1,25},{9,1},{17,9},{25,17},{2,26},{10... | collective-permute-start | bytes 983048 | tf_op jit(solution)/shard_map/ppermute | solution.py:466
  170.5 9.6 %collective-permute-start.33 = (f32[8,5,16,128]{3,2,1,0:T(8,128)S(1)}, f32[8,5,16,128]{3,2,1,0:T(8,128)S(1)}, u32[]{:S(2)}, u32[]{:S(2)}) collective-permute-start(f32[8,5,16,128]{3,2,1,0:T(8,128)S(1)} %get-tuple-element.279), channel_id=1, source_target_pairs={{0,1},{1,0},{2,3},{3,2},{4,5},{5,4},{6,7},{7,6},{8,9},{9,8},{10,11... | collective-permute-start | bytes 983048 | tf_op jit(solution)/shard_map/ppermute | solution.py:358
  181.0 15.7 %collective-permute-start.35 = (f32[4,5,32,128]{3,2,1,0:T(8,128)S(1)}, f32[4,5,32,128]{3,2,1,0:T(8,128)S(1)}, u32[]{:S(2)}, u32[]{:S(2)}) collective-permute-start(f32[4,5,32,128]{3,2,1,0:T(8,128)S(1)} %get-tuple-element.289), channel_id=1, source_target_pairs={{0,8},{8,16},{16,24},{24,0},{1,9},{9,17},{17,25},{25,1},{2,10},{10... | collective-permute-start | bytes 983048 | tf_op jit(solution)/shard_map/ppermute | solution.py:466
  183.4 13.3 %collective-permute-start.36 = (f32[4,5,32,128]{3,2,1,0:T(8,128)S(1)}, f32[4,5,32,128]{3,2,1,0:T(8,128)S(1)}, u32[]{:S(2)}, u32[]{:S(2)}) collective-permute-start(f32[4,5,32,128]{3,2,1,0:T(8,128)S(1)} %get-tuple-element.290), channel_id=1, source_target_pairs={{0,16},{8,24},{16,0},{24,8},{1,17},{9,25},{17,1},{25,9},{2,18},{10... | collective-permute-start | bytes 983048 | tf_op jit(solution)/shard_map/ppermute | solution.py:466
  183.8 12.9 %collective-permute-start.41 = (f32[16,5,8,128]{3,2,1,0:T(8,128)S(1)}, f32[16,5,8,128]{3,2,1,0:T(8,128)S(1)}, u32[]{:S(2)}, u32[]{:S(2)}) collective-permute-start(f32[16,5,8,128]{3,2,1,0:T(8,128)S(1)} %get-tuple-element.297), channel_id=1, source_target_pairs={{2,0},{3,1},{4,6},{5,7},{10,8},{11,9},{12,14},{13,15},{18,16},{19,... | collective-permute-start | bytes 983048 | tf_op jit(solution)/shard_map/ppermute | solution.py:350
  185.1 12.8 %collective-permute-start.37 = (f32[4,5,32,128]{3,2,1,0:T(8,128)S(1)}, f32[4,5,32,128]{3,2,1,0:T(8,128)S(1)}, u32[]{:S(2)}, u32[]{:S(2)}) collective-permute-start(f32[4,5,32,128]{3,2,1,0:T(8,128)S(1)} %get-tuple-element.291), channel_id=1, source_target_pairs={{0,24},{8,0},{16,8},{24,16},{1,25},{9,1},{17,9},{25,17},{2,26},{10... | collective-permute-start | bytes 983048 | tf_op jit(solution)/shard_map/ppermute | solution.py:466
  186.4 11.5 %collective-permute-start.40 = (f32[8,5,16,128]{3,2,1,0:T(8,128)S(1)}, f32[8,5,16,128]{3,2,1,0:T(8,128)S(1)}, u32[]{:S(2)}, u32[]{:S(2)}) collective-permute-start(f32[8,5,16,128]{3,2,1,0:T(8,128)S(1)} %get-tuple-element.302), channel_id=1, source_target_pairs={{0,1},{1,0},{2,3},{3,2},{4,5},{5,4},{6,7},{7,6},{8,9},{9,8},{10,11... | collective-permute-start | bytes 983048 | tf_op jit(solution)/shard_map/ppermute | solution.py:358
  198.8 9.3 %collective-permute-start.42 = (f32[4,5,32,128]{3,2,1,0:T(8,128)S(1)}, f32[4,5,32,128]{3,2,1,0:T(8,128)S(1)}, u32[]{:S(2)}, u32[]{:S(2)}) collective-permute-start(f32[4,5,32,128]{3,2,1,0:T(8,128)S(1)} %get-tuple-element.314), channel_id=1, source_target_pairs={{0,8},{8,16},{16,24},{24,0},{1,9},{9,17},{17,25},{25,1},{2,10},{10... | collective-permute-start | bytes 983048 | tf_op jit(solution)/shard_map/ppermute | solution.py:466
  199.4 10.6 %collective-permute-start.43 = (f32[4,5,32,128]{3,2,1,0:T(8,128)S(1)}, f32[4,5,32,128]{3,2,1,0:T(8,128)S(1)}, u32[]{:S(2)}, u32[]{:S(2)}) collective-permute-start(f32[4,5,32,128]{3,2,1,0:T(8,128)S(1)} %get-tuple-element.315), channel_id=1, source_target_pairs={{0,16},{8,24},{16,0},{24,8},{1,17},{9,25},{17,1},{25,9},{2,18},{10... | collective-permute-start | bytes 983048 | tf_op jit(solution)/shard_map/ppermute | solution.py:466
  201.1 12.7 %collective-permute-start.44 = (f32[4,5,32,128]{3,2,1,0:T(8,128)S(1)}, f32[4,5,32,128]{3,2,1,0:T(8,128)S(1)}, u32[]{:S(2)}, u32[]{:S(2)}) collective-permute-start(f32[4,5,32,128]{3,2,1,0:T(8,128)S(1)} %get-tuple-element.316), channel_id=1, source_target_pairs={{0,24},{8,0},{16,8},{24,16},{1,25},{9,1},{17,9},{25,17},{2,26},{10... | collective-permute-start | bytes 983048 | tf_op jit(solution)/shard_map/ppermute | solution.py:466
  201.2 6.6 %collective-permute-start.45 = (f32[8,5,8,128]{3,2,1,0:T(8,128)S(1)}, f32[8,5,8,128]{3,2,1,0:T(8,128)S(1)}, u32[]{:S(2)}, u32[]{:S(2)}) collective-permute-start(f32[8,5,8,128]{3,2,1,0:T(8,128)S(1)} %get-tuple-element.317), channel_id=1, source_target_pairs={{0,1},{1,0},{2,3},{3,2},{4,5},{5,4},{6,7},{7,6},{8,9},{9,8},{10,11... | collective-permute-start | bytes 491528 | tf_op jit(solution)/shard_map/ppermute | solution.py:358
  214.7 6.6 %collective-permute-start.46 = (f32[4,5,16,128]{3,2,1,0:T(8,128)S(1)}, f32[4,5,16,128]{3,2,1,0:T(8,128)S(1)}, u32[]{:S(2)}, u32[]{:S(2)}) collective-permute-start(f32[4,5,16,128]{3,2,1,0:T(8,128)S(1)} %get-tuple-element.339), channel_id=1, source_target_pairs={{0,8},{8,16},{16,24},{24,0},{1,9},{9,17},{17,25},{25,1},{2,10},{10... | collective-permute-start | bytes 491528 | tf_op jit(solution)/shard_map/ppermute | solution.py:466
  216.8 6.4 %collective-permute-start.47 = (f32[4,5,16,128]{3,2,1,0:T(8,128)S(1)}, f32[4,5,16,128]{3,2,1,0:T(8,128)S(1)}, u32[]{:S(2)}, u32[]{:S(2)}) collective-permute-start(f32[4,5,16,128]{3,2,1,0:T(8,128)S(1)} %get-tuple-element.340), channel_id=1, source_target_pairs={{0,16},{8,24},{16,0},{24,8},{1,17},{9,25},{17,1},{25,9},{2,18},{10... | collective-permute-start | bytes 491528 | tf_op jit(solution)/shard_map/ppermute | solution.py:466
  217.1 7.1 %collective-permute-start.48 = (f32[4,5,16,128]{3,2,1,0:T(8,128)S(1)}, f32[4,5,16,128]{3,2,1,0:T(8,128)S(1)}, u32[]{:S(2)}, u32[]{:S(2)}) collective-permute-start(f32[4,5,16,128]{3,2,1,0:T(8,128)S(1)} %get-tuple-element.341), channel_id=1, source_target_pairs={{0,24},{8,0},{16,8},{24,16},{1,25},{9,1},{17,9},{25,17},{2,26},{10... | collective-permute-start | bytes 491528 | tf_op jit(solution)/shard_map/ppermute | solution.py:466
  (15 other events, 212.4 us)
